TPU v7x, 128 devices: a whole 4x4x4 slice. The times are simulated.
128 devices in a mesh: grp: 8 (over y, core), dp: 16 (over x, z).
Axes of the slice: x: 4, y: 4, z: 4, core: 2. Of those that a mesh axis runs over, the one named last changes fastest.
Arguments:
- query_lat: bfloat16 [256, 32, 64, 512], P(('grp', 'dp')), parts along dimension 0, may hold values from -6 to 6
- query_rope: bfloat16 [256, 32, 4096], P(('grp', 'dp')), parts along dimension 0, may hold values from -400 to 400
- lat_cache: bfloat16 [256, 2048, 512], P(('grp', 'dp')), parts along dimension 0, may hold values from -40 to 40
- rope_cache: bfloat16 [256, 64, 2048], P(('grp', 'dp')), parts along dimension 0, may hold values from -8 to 8
- new_lat: bfloat16 [256, 32, 512], P(('grp', 'dp')), parts along dimension 0, may hold values from -6 to 6
- new_rope: bfloat16 [256, 32, 64], P(('grp', 'dp')), parts along dimension 0, may hold values from -6 to 6
- cache_len: int32 [256], P(('grp', 'dp')), parts along dimension 0, may hold values from 2 to 2048, as said below
- live_rows: int32 [256], P(('grp', 'dp')), parts along dimension 0, may hold values from 1 to 32, as said below
- ancestors: int32 [256, 32, 32], P(('grp', 'dp')), parts along dimension 0, may hold values from 0 to 1, as said below
- value_up: bfloat16 [64, 512, 128], P('dp'), may hold values from -0.25 to 0.25
- out_proj: bfloat16 [8192, 7168], P('dp'), may hold values from -0.0625 to 0.0625
Outputs:
- attn_out: bfloat16 [8192, 7168], P(('grp', 'dp')), parts along dimension 0
There are 8 independent parts, one for each index of `grp`. A program takes and returns all parts, laid end to end along the dimension named above; an argument that names none is the same for every part. Nothing has to cross between parts.
Inputs may be any that keep to these rules, and one draw needn't show every extreme that they name: `cache_len`: at least 2; the largest equals 2048 in every draw. `live_rows`: the largest equals 32 in every draw. ancestors[r, i, j] is 1 exactly when tree row j is row i or an ancestor of it; row 0 is the root and every ancestor of row i has a smaller index.
All inputs are finite; a program needn't handle non-finite values.
Results may differ from a plain program's by a relative error of at most 0.02.
Values may be sent and summed in bfloat16 or wider, within the bound.
A program may use at most 128 MiB of HBM per device.

v0:
```python
import jax
import jax.numpy as jnp
from jax import lax
from jax.sharding import PartitionSpec as P

score_scale = 192.0 ** (-0.5)
very_negative = -1e30


def absorb_block(carry_state, query_rows, rope_rows, key_rows, rope_keys, value_rows, valid_mask):
    running_top, running_total, summed = carry_state
    scores = (
        jnp.einsum("nc,pc->np", query_rows, key_rows, preferred_element_type=jnp.float32)
        + jnp.dot(rope_rows, rope_keys, preferred_element_type=jnp.float32)
    ) * score_scale
    new_top = jnp.maximum(
        running_top, jnp.max(jnp.where(valid_mask, scores, very_negative), axis=1)
    )
    rescale = jnp.exp(running_top - new_top)
    weights = jnp.where(valid_mask, jnp.exp(scores - new_top[:, None]), 0.0)
    running_total = running_total * rescale + jnp.sum(weights, axis=1)
    summed = summed * rescale[:, None] + jnp.dot(
        weights.astype(jnp.bfloat16), value_rows, preferred_element_type=jnp.float32
    )
    return (new_top, running_total, summed)


def start_state(row_count, latent_width):
    return (
        jnp.full((row_count,), very_negative, jnp.float32),
        jnp.zeros((row_count,), jnp.float32),
        jnp.zeros((row_count, latent_width), jnp.float32),
    )


def cache_part(
    carry_state, query_rows, rope_rows, lat_cache, rope_cache, length, first_block, last_block
):
    block_size = min(512, lat_cache.shape[0] // 4)

    def block_step(index_block, inner_state):
        offset = index_block * block_size
        key_rows = lax.dynamic_slice_in_dim(lat_cache, offset, block_size, 0)
        rope_block = lax.dynamic_slice_in_dim(rope_cache, offset, block_size, 1)
        position = offset + lax.broadcasted_iota(jnp.int32, (1, block_size), 1)
        return absorb_block(
            inner_state, query_rows, rope_rows, key_rows, rope_block, key_rows, position < length
        )

    return lax.fori_loop(first_block, last_block, block_step, carry_state)


def block_count(length, lat_cache):
    block_size = min(512, lat_cache.shape[0] // 4)
    return (length + block_size - 1) // block_size


def flat_queries(query_lat, query_rope):
    tree_rows, heads, latent_width = query_lat.shape
    return (
        query_lat.reshape(tree_rows * heads, latent_width),
        query_rope.reshape(tree_rows * heads, -1),
    )


def tree_part(carry_state, query_rows, rope_rows, new_lat, new_rope, ancestors, heads):
    valid_mask = jnp.repeat(ancestors > 0, heads, axis=0)
    return absorb_block(
        carry_state, query_rows, rope_rows, new_lat, new_rope.T, new_lat, valid_mask
    )


def finish(carry_state, live, tree_rows, heads):
    running_top, running_total, summed = carry_state
    context = summed / running_total[:, None]
    alive = lax.broadcasted_iota(jnp.int32, (tree_rows * heads, 1), 0) // heads < live
    return jnp.where(alive, context, 0.0).astype(jnp.bfloat16).reshape(tree_rows, heads, -1)


def per_device(
    query_lat,
    query_rope,
    lat_cache,
    rope_cache,
    new_lat,
    new_rope,
    cache_len,
    live_rows,
    ancestors,
    value_up,
    out_proj,
):
    local_requests, tree_rows, heads, latent_width = query_lat.shape
    row_count = tree_rows * heads
    contexts = []
    for request in range(local_requests):
        query_rows, rope_rows = flat_queries(query_lat[request], query_rope[request])
        carry_state = tree_part(
            start_state(row_count, latent_width),
            query_rows,
            rope_rows,
            new_lat[request],
            new_rope[request],
            ancestors[request],
            heads,
        )
        carry_state = cache_part(
            carry_state,
            query_rows,
            rope_rows,
            lat_cache[request],
            rope_cache[request],
            cache_len[request],
            0,
            block_count(cache_len[request], lat_cache[request]),
        )
        contexts.append(finish(carry_state, live_rows[request], tree_rows, heads))
    context = jnp.concatenate(contexts, axis=0)
    exchanged = lax.all_to_all(context, "dp", split_axis=1, concat_axis=0, tiled=True)
    head_values = jnp.einsum(
        "nhc,hcv->nhv", exchanged, value_up, preferred_element_type=jnp.float32
    ).astype(jnp.bfloat16)
    flat_values = head_values.reshape(head_values.shape[0], -1)
    return lax.psum_scatter(
        jnp.dot(flat_values, out_proj, preferred_element_type=jnp.float32).astype(jnp.bfloat16),
        "dp",
        scatter_dimension=0,
        tiled=True,
    )


def solution(mesh):
    in_specs = (
        P(("grp", "dp"), None, None, None),
        P(("grp", "dp"), None, None),
        P(("grp", "dp"), None, None),
        P(("grp", "dp"), None, None),
        P(("grp", "dp"), None, None),
        P(("grp", "dp"), None, None),
        P(("grp", "dp")),
        P(("grp", "dp")),
        P(("grp", "dp"), None, None),
        P("dp", None, None),
        P("dp", None),
    )
    out_specs = P(("grp", "dp"), None)
    return jax.shard_map(
        per_device, mesh=mesh, in_specs=in_specs, out_specs=out_specs, check_vma=False
    )
```

profile of v0, /device:TPU:0, one launch (start us, length us, event | category | flops | bytes accessed | tf_op | source)
XLA Modules:
  0.0 295.1 jit_solution(3988118609879491333)
XLA Ops:
  6.5 1.3 fusion.68
  9.1 1.3 fusion.50
  10.4 0.1 copy.24
  10.5 0.2 broadcast_in_dim.78
  10.7 0.4 reshape.95
  11.1 4.2 %fusion.65 = (bf16[1,32,64,512]{3,2,1,0:T(8,128)(2,1)S(1)}, bf16[1,32,64,512]{3,2,1,0:T(8,128)(2,1)}) fusion(bf16[2,32,64,512]{3,2,1,0:T(8,128)(2,1)} %param.15), kind=kLoop, calls=%fused_computation.102 | loop fusion | bytes 8388608 | tf_op jit(solution)/shard_map/slice | solution.py:97
  15.3 0.8 fusion.66
  16.1 0.5 reshape_squeeze.13
  16.7 0.7 fusion.44
  17.4 1.4 select_reduce_fusion.3
  18.9 2.7 convolution_add_fusion.1
  21.6 1.6 slice_bitcast_fusion.1
  23.2 0.7 slice_bitcast_fusion.3
  23.9 13.1 %while.28 = (s32[]{:T(128)}, f32[2048]{0:T(1024)S(1)}, f32[2048]{0:T(1024)S(1)}, f32[2048,512]{1,0:T(8,128)}, s32[]{:T(128)}, /*index=5*/s32[]{:T(128)}, bf16[20...) while((s32[]{:T(128)}, f32[2048]{0:T(1024)S(1)}, ...), condition=%wide.region_5.6_spmd, body=%wide.region_2.5_spmd.sunk | while | flops 2294289408 | bytes 66521344 | solution.py:50
  23.9 3.1 %fusion.100 = f32[512,2048]{1,0:T(8,128)S(1)} fusion(bf16[2048,512]{1,0:T(8,128)(2,1)} %get-tuple-element.404, bf16[2048,512]{1,0:T(8,128)(2,1)} %get-tuple-element.403, s32[]{:T(128)S(6)} %select_n.124), kind=kOutput, calls=%fused_computation.10.clone.1 | convolution fusion | flops 1073741824 | bytes 6815748 | tf_op jit(solution)/shard_map/while/body/nc,pc->np/dot_general | solution.py:13
  27.0 0.6 add_compare_fusion.4
  27.6 2.0 select_reduce_fusion.6
  29.6 0.7 fusion.101
  30.3 1.4 copy-done.1
  31.8 3.4 %multiply_add_fusion.9 = f32[2048,512]{1,0:T(8,128)S(1)} fusion(f32[2048,512]{1,0:T(8,128)S(1)} %copy-done.1, f32[512,2048]{1,0:T(8,128)S(1)} %get-tuple-element.310, f32[2048]{0:T(1024)S(1)} %get-tuple-element.312, f32[2048]{0:T(1024)S(1)} %max.8, pred[512]{0:T(512)(128)(4,1)S(1)} %add_compare_fusion.4, bf16[2048,512]{1,0:T(8,128)(2,1)} %get-tuple-element.403, ...), kind=kOutput, calls=%fused_computation.clone.1 | convolution fusion | flops 1078984704 | bytes 13124100 | tf_op jit(solution)/shard_map/while/body/dot_general | solution.py:22
  35.1 1.9 copy-done.2
  37.1 0.5 fusion.67
  37.6 1.2 fusion.55
  38.9 0.2 broadcast_in_dim.82
  39.1 0.4 reshape.97
  39.5 3.0 %fusion.41 = f32[2048,32]{0,1:T(8,128)} fusion(bf16[2048,512]{1,0:T(8,128)(2,1)} %bitcast.75, bf16[2,32,512]{2,1,0:T(8,128)(2,1)S(1)} %copy-done.10), kind=kOutput, calls=%fused_computation.68 | convolution fusion | flops 67108864 | bytes 2392064 | tf_op jit(solution)/shard_map/nc,pc->np/dot_general | solution.py:13
  42.5 1.5 reshape_squeeze.15
  44.0 1.3 select_reduce_fusion.2
  45.4 3.5 %convolution_add_fusion = f32[2048,512]{1,0:T(8,128)} fusion(f32[2048]{0:T(1024)S(1)} %get-tuple-element.177, pred[2048,32]{0,1:T(32,128)(4,1)S(1)} %reshape.97, f32[2048,32]{0,1:T(8,128)S(1)} %get-tuple-element.184, f32[2048]{0:T(1024)S(1)} %broadcast_maximum_fusion, bf16[2,32,512]{2,1,0:T(8,128)(2,1)} %param.19), kind=kOutput, calls=%fused_computation.44 | convolution fusion | flops 68354048 | bytes 4571136 | tf_op jit(solution)/shard_map/dot_general | solution.py:22
  48.9 11.2 %while.29 = (s32[]{:T(128)}, f32[2048]{0:T(1024)S(1)}, f32[2048]{0:T(1024)S(1)}, f32[2048,512]{1,0:T(8,128)}, s32[]{:T(128)}, /*index=5*/s32[]{:T(128)}, bf16[20...) while((s32[]{:T(128)}, f32[2048]{0:T(1024)S(1)}, ...), condition=%wide.region_11.12_spmd, body=%wide.region_8.11_spmd.sunk | while | flops 2294289408 | bytes 66783488 | solution.py:50
  48.9 2.9 fusion.107
  51.7 0.6 add_compare_fusion.5
  52.4 1.1 select_reduce_fusion.7
  53.6 0.7 fusion.108
  54.3 1.4 copy-done.3
  55.7 2.3 multiply_add_fusion.11
  58.1 2.0 copy-done.4
  60.0 0.7 fusion.54
  60.7 2.7 select_convert_fusion.1
  63.5 0.7 select_convert_fusion
  64.2 0.4 pad_maximum_fusion
  64.6 2.3 copy.26
  66.9 107.9 %all_to_all.18 = bf16[64,64,512]{2,0,1:T(8,128)(2,1)S(1)} all-to-all(bf16[64,64,512]{2,0,1:T(8,128)(2,1)S(1)} %copy.26), channel_id=1, replica_groups=mesh['grp'=8,'dp'=16] {'dp'}, dimensions={1} | all-to-all | bytes 8388608 | tf_op jit(solution)/shard_map/all_to_all | solution.py:119
  174.8 0.5 copy.27
  175.3 1.5 convolution_convert_fusion.1
  176.8 0.2 slice-done.1
  177.0 11.2 %convolution_convert_fusion = bf16[1024,7168]{1,0:T(8,128)(2,1)} fusion(bf16[1024,512]{0,1:T(8,128)(2,1)S(1)} %bitcast.79, bf16[512,7168]{1,0:T(8,128)(2,1)S(1)} %bitcast.81), kind=kOutput, calls=%fused_computation.40 | convolution fusion | flops 7523532800 | bytes 23068672 | tf_op jit(solution)/shard_map/dot_general | solution.py:125
  188.2 100.0 %reduce-scatter.2.cloned.1.call-done = bf16[64,7168]{1,0:T(8,128)(2,1)} async-done(((bf16[1024,7168]{1,0:T(8,128)(2,1)}), bf16[64,7168]{1,0:T(8,128)(2,1)}) %reduce-scatter.2.cloned.1.call-update) | async-done | bytes 917520 | tf_op jit(solution)/shard_map/reduce_scatter | solution.py:124
  (43 shorter events, 0.4 us)
Async XLA Ops:
  6.5 168.8 %copy-start = (bf16[4,512,128]{2,1,0:T(8,128)(2,1)S(1)}, bf16[4,512,128]{2,1,0:T(8,128)(2,1)}, u32[]{:S(2)}) copy-start(bf16[4,512,128]{2,1,0:T(8,128)(2,1)} %param.24) | copy-start | bytes 1572868
  6.5 281.7 %reduce-scatter.2.cloned.1.call-start = ((), (), s32[]{:S(2)}) async-start(), calls=%async_computation.2 | async-start | bytes 15597568 | tf_op jit(solution)/shard_map/reduce_scatter | solution.py:124
  11.1 4.2 %copy-start.8 = (bf16[2,32,4096]{2,1,0:T(8,128)(2,1)S(1)}, bf16[2,32,4096]{2,1,0:T(8,128)(2,1)}, u32[]{:S(2)}) copy-start(bf16[2,32,4096]{2,1,0:T(8,128)(2,1)} %param.16) | copy-start | bytes 1572868
  11.1 5.5 %copy-start.10 = (bf16[2,32,512]{2,1,0:T(8,128)(2,1)S(1)}, bf16[2,32,512]{2,1,0:T(8,128)(2,1)}, u32[]{:S(2)}) copy-start(bf16[2,32,512]{2,1,0:T(8,128)(2,1)} %param.19) | copy-start | bytes 196612
  15.3 3.6 %copy-start.6 = (bf16[1,32,64,512]{3,2,1,0:T(8,128)(2,1)}, bf16[1,32,64,512]{3,2,1,0:T(8,128)(2,1)S(1)}, u32[]{:S(2)}) copy-start(bf16[1,32,64,512]{3,2,1,0:T(8,128)(2,1)S(1)} %get-tuple-element.167) | copy-start | bytes 6291460
  16.6 4.9 %copy-start.7 = (bf16[2,2048,512]{2,1,0:T(8,128)(2,1)S(1)}, bf16[2,2048,512]{2,1,0:T(8,128)(2,1)}, u32[]{:S(2)}) copy-start(bf16[2,2048,512]{2,1,0:T(8,128)(2,1)} %param.17) | copy-start | bytes 12582916
  21.6 1.6 copy-start.9
  23.9 13.1 %copy-start.13 = (s32[2]{0:T(128)S(1)}, s32[2]{0:T(128)}, u32[]{:S(2)}) copy-start(s32[2]{0:T(128)} %param.22) | copy-start | bytes 28
  23.9 14.9 %copy-start.11 = (pred[32,32]{1,0:T(8,128)(4,1)S(1)}, pred[32,32]{1,0:T(8,128)(4,1)}, u32[]{:S(2)}) copy-start(pred[32,32]{1,0:T(8,128)(4,1)} %get-tuple-element.174) | copy-start | bytes 3076
  29.6 2.2 copy-start.1
  35.1 2.0 copy-start.2
  48.9 11.9 %copy-start.12 = (pred[2048]{0:T(1024)(128)(4,1)S(1)}, pred[2048]{0:T(1024)(128)(4,1)}, u32[]{:S(2)}) copy-start(pred[2048]{0:T(1024)(128)(4,1)} %fusion.55) | copy-start | bytes 6148
  53.5 2.2 copy-start.3
  58.1 2.0 copy-start.4
  60.0 3.5 %copy-start.5 = (f32[2048,512]{1,0:T(8,128)S(1)}, f32[2048,512]{1,0:T(8,128)}, u32[]{:S(2)}) copy-start(f32[2048,512]{1,0:T(8,128)} %get-tuple-element.115) | copy-start | bytes 12582916
  66.9 109.9 %slice-start = ((s8[7340032]{0:T(1024)(128)(4,1)}), s8[3145728]{0:T(1024)(128)(4,1)S(1)}, s32[]{:S(2)}) async-start(s8[7340032]{0:T(1024)(128)(4,1)} %bitcast.80), calls=%async_computation.3 | async-start | bytes 6291456
  174.8 2.2 slice-start.1
Sparse Core Ops, SparseCore 0:
  188.3 99.8 reduce-scatter.1
where the time goes:
time: 297 us; the launch traced here: 295 us
  blocking collectives  108 us (36%)
  waiting for transfers between devices  100 us (34%)
  matrix products  40 us (13%)
  local copies, waits for them, and re-layouts  22.4 us (8%)
  between operations  14.8 us (5%)
  other arithmetic  9.85 us (3%)
    all_to_all x1, blocking collectives, per_device(): lax.all_to_all(context, 'dp', split_axis=1, concat_axis=0, tiled=True)  108 us
    reduce_scatter x1, waiting for transfers between devices, per_device(): lax.psum_scatter(jnp.dot(flat_values, out_proj, preferred_element_type=jn...  100 us
    dot_general x4, matrix products, absorb_block(): jnp.dot(weights.astype(jnp.bfloat16), value_rows, preferred_element_type=...  11.9 us
    dot_general x1, matrix products, per_device(): jnp.dot(flat_values, out_proj, preferred_element_type=jnp.float32)  11.2 us
    dot_general x4, matrix products, absorb_block(): jnp.einsum('nc,pc->np', query_rows, key_rows, preferred_element_type=jnp....  9.65 us
    while x10, local copies, waits for them, and re-layouts  6.75 us
  transfers between devices with their start and end apart: 1, of which 1 were waited for; matrix products, arithmetic and copies ran while one was open for 0% of the time, Pallas kernels for 0%

commit v1 on v0

v1 whole, which is shorter than its diff:
```python
import functools
import jax
import jax.numpy as jnp
from jax import lax
from jax.experimental import pallas as pl
from jax.experimental.pallas import tpu as pltpu
from jax.sharding import PartitionSpec as P

score_scale = 192.0 ** (-0.5)
log2_e = 1.4426950408889634
very_negative = -1e30


def attend_kernel(
    rows_blk, key_blk, halves,
    len_ref, live_ref,
    q_ref, qr_ref, lat_ref, rope_ref, new_ref, newr_ref, anc_ref,
    out_ref, top_s, tot_s, acc_s,
):
    request = pl.program_id(0)
    length, live = len_ref[request], live_ref[request]
    heads = q_ref.shape[2]
    width = q_ref.shape[3]
    nrow = rows_blk * heads
    sub = nrow // halves
    sub_rows = rows_blk // halves
    factor = score_scale * log2_e
    nt = (((1,), (1,)), ((), ()))

    def scores_of(queries, ropes, keys, rope_keys):
        s = lax.dot_general(queries, keys, nt, preferred_element_type=jnp.float32)
        s = s + jnp.dot(ropes, rope_keys, preferred_element_type=jnp.float32)
        return s * factor

    def lane_sum(w):
        n = w.shape[1]
        parts = [w[:, c * 128:(c + 1) * 128] for c in range(n // 128)]
        while len(parts) > 1:
            parts = [a + b for a, b in zip(parts[::2], parts[1::2])] + (parts[-1:] if len(parts) % 2 else [])
        return parts[0]

    def queries_of(base, half):
        row0 = base + half * sub_rows
        q = q_ref[0, pl.ds(row0, sub_rows)].reshape(sub, width)
        qr = qr_ref[0, pl.ds(pl.multiple_of(row0 * heads, 8), sub), :]
        return q, qr

    def tree_step(base):
        for half in range(halves):
            q, qr = queries_of(base, half)
            row0 = base + half * sub_rows
            s = lax.dot_general(q, new_ref[0], nt, preferred_element_type=jnp.float32)
            s = s + lax.dot_general(qr, newr_ref[0], nt, preferred_element_type=jnp.float32)
            s = s * factor
            anc = anc_ref[0, pl.ds(row0, sub_rows), :]
            n = anc.shape[1]
            bias = jnp.where(anc > 0, 0.0, very_negative)
            s = (s.reshape(sub_rows, heads, n) + bias[:, None, :]).reshape(sub, n)
            top = jnp.max(s, axis=1, keepdims=True)
            w = jnp.exp2(s - top)
            rows = pl.ds(half * sub, sub)
            top_s[rows, :] = jnp.broadcast_to(top, (sub, 128))
            tot_s[rows, :] = jnp.sum(w, axis=1, keepdims=True) * jnp.where(
                lax.broadcasted_iota(jnp.int32, (1, 128), 1) == 0, 1.0, 0.0)
            acc_s[rows, :] = jnp.dot(w.astype(jnp.bfloat16), new_ref[0], preferred_element_type=jnp.float32)

    def cache_step(base, offset, size, masked):
        keys = lat_ref[0, pl.ds(offset, size), :]
        rope_keys = rope_ref[0, :, pl.ds(offset, size)]
        for half in range(halves):
            q, qr = queries_of(base, half)
            s = scores_of(q, qr, keys, rope_keys)
            if masked:
                position = offset + lax.broadcasted_iota(jnp.int32, (1, size), 1)
                s = jnp.where(position < length, s, very_negative)
            rows = pl.ds(half * sub, sub)
            old = top_s[rows, :]
            new = jnp.maximum(old, jnp.max(s, axis=1, keepdims=True))
            rescale = jnp.exp2(old - new)
            w = jnp.exp2(s - new[:, :1])
            tot_s[rows, :] = tot_s[rows, :] * rescale + lane_sum(w)
            top_s[rows, :] = new
            acc_s[rows, :] = acc_s[rows, :] * rescale[:, :1] + jnp.dot(
                w.astype(jnp.bfloat16), keys, preferred_element_type=jnp.float32)

    full = length // key_blk
    rest = length - full * key_blk
    tail = pl.multiple_of(full * key_blk, key_blk)

    def row_block(index, carry):
        base = index * rows_blk
        tree_step(base)

        def key_step(k, c):
            cache_step(base, pl.multiple_of(k * key_blk, key_blk), key_blk, False)
            return c

        lax.fori_loop(0, full, key_step, 0)

        @pl.when(rest > key_blk // 2)
        def _():
            cache_step(base, tail, key_blk, True)

        @pl.when(jnp.logical_and(rest > 0, rest <= key_blk // 2))
        def _():
            cache_step(base, tail, key_blk // 2, True)

        for half in range(halves):
            rows = pl.ds(half * sub, sub)
            total = jnp.sum(tot_s[rows, :], axis=1, keepdims=True)
            ctx = acc_s[rows, :] * (1.0 / total)
            row0 = base + half * sub_rows
            alive = row0 + lax.broadcasted_iota(jnp.int32, (sub_rows, heads, 1), 0) < live
            ctx = jnp.where(alive, ctx.reshape(sub_rows, heads, width), 0.0)
            out_ref[0, pl.ds(row0, sub_rows)] = ctx.astype(out_ref.dtype)
        return carry

    blocks = (live + rows_blk - 1) // rows_blk
    lax.fori_loop(0, blocks, row_block, 0)

    def clear(index, carry):
        out_ref[0, pl.ds(index * rows_blk, rows_blk)] = jnp.zeros((rows_blk, heads, width), out_ref.dtype)
        return carry

    lax.fori_loop(blocks, q_ref.shape[1] // rows_blk, clear, 0)


def attend(query_lat, query_rope, lat_cache, rope_cache, new_lat, new_rope, cache_len, live_rows, ancestors,
           rows_blk=8, key_blk=512, halves=2):
    reqs, rows, heads, width = query_lat.shape
    ropes = query_rope.reshape(reqs, rows * heads, -1)
    nrow = rows_blk * heads

    def whole(x):
        nd = x.ndim
        return pl.BlockSpec((1,) + x.shape[1:], lambda r, *_: (r,) + (0,) * (nd - 1))

    args = (query_lat, ropes, lat_cache, rope_cache, new_lat, new_rope, ancestors)
    return pl.pallas_call(
        functools.partial(attend_kernel, rows_blk, key_blk, halves),
        grid_spec=pltpu.PrefetchScalarGridSpec(
            num_scalar_prefetch=2,
            grid=(reqs,),
            in_specs=[whole(x) for x in args],
            out_specs=whole(query_lat),
            scratch_shapes=[
                pltpu.VMEM((nrow, 128), jnp.float32),
                pltpu.VMEM((nrow, 128), jnp.float32),
                pltpu.VMEM((nrow, width), jnp.float32),
            ],
        ),
        out_shape=jax.ShapeDtypeStruct(query_lat.shape, jnp.bfloat16),
        compiler_params=pltpu.CompilerParams(vmem_limit_bytes=48 * 2**20),
        cost_estimate=pl.CostEstimate(flops=13 * 10**9, bytes_accessed=14 * 2**20, transcendentals=6 * 2**20),
    )(cache_len, live_rows, *args)


def per_device(query_lat, query_rope, lat_cache, rope_cache, new_lat, new_rope, cache_len, live_rows, ancestors,
               value_up, out_proj):
    all_up = lax.all_gather(value_up, "dp", axis=0, tiled=True)
    context = attend(query_lat, query_rope, lat_cache, rope_cache, new_lat, new_rope, cache_len, live_rows, ancestors)
    reqs, rows, heads, width = context.shape
    context = context.reshape(reqs * rows, heads, width)
    head_values = jnp.einsum("nhc,hcv->nhv", context, all_up, preferred_element_type=jnp.float32).astype(jnp.bfloat16)
    exchanged = lax.all_to_all(head_values, "dp", split_axis=1, concat_axis=0, tiled=True)
    flat_values = exchanged.reshape(exchanged.shape[0], -1)
    return lax.psum_scatter(
        jnp.dot(flat_values, out_proj, preferred_element_type=jnp.float32).astype(jnp.bfloat16),
        "dp", scatter_dimension=0, tiled=True)


def solution(mesh):
    both = ("grp", "dp")
    in_specs = (
        P(both, None, None, None), P(both, None, None), P(both, None, None), P(both, None, None),
        P(both, None, None), P(both, None, None), P(both), P(both), P(both, None, None),
        P("dp", None, None), P("dp", None),
    )
    return jax.shard_map(per_device, mesh=mesh, in_specs=in_specs, out_specs=P(both, None), check_vma=False)
```

time: 297 us -> 234 us (0.79)
  blocking collectives: 108 us -> 21.9 us
  waiting for transfers between devices: 100 us -> 144 us
  Pallas kernels: 0 us -> 23.4 us
  matrix products: 40 us -> 20.8 us
  local copies, waits for them, and re-layouts: 22.4 us -> 9.56 us
  other arithmetic: 9.85 us -> 0 us
    all_to_all x1, blocking collectives: 108 us -> 21.9 us  [per_device(): lax.all_to_all(head_values, 'dp', split_axis=1, concat_axis=0, tiled=True)]
    all_gather x0 -> x1, waiting for transfers between devices: none -> 43.6 us  [per_device(): all_up = lax.all_gather(value_up, 'dp', axis=0, tiled=True)]
    pallas_call x0 -> x1, Pallas kernels: none -> 23.4 us  [attend(): pl.pallas_call(functools.partial(attend_kernel, rows_blk, key_blk, halves...]
    dot_general x13 -> x1, matrix products: 28.8 us -> 9.73 us  [per_device(): jnp.einsum('nhc,hcv->nhv', context, all_up, preferred_element_type=jnp.fl...]
    slice x4 -> x0, local copies, waits for them, and re-layouts: 6.84 us -> none  [the longest x1 4.15 us: per_device(): query_lat[request]]
    while x10 -> x0, local copies, waits for them, and re-layouts: 6.75 us -> none
    unnamed x24 -> x16, local copies, waits for them, and re-layouts: 0.22 us -> 6.62 us
    convert_element_type x2 -> x0, other arithmetic: 3.43 us -> none  [finish(): jnp.where(alive, context, 0.0).astype(jnp.bfloat16)]
  transfers between devices with their start and end apart: 1 -> 2, of which waited for: 1 -> 2; matrix products, arithmetic and copies ran while one was open for 0% -> 1% of each run, Pallas kernels for 0% -> 10%
where the time goes in v1:
time: 234 us; the launch traced here: 233 us
  waiting for transfers between devices  144 us (62%)
  Pallas kernels  23.4 us (10%)
  blocking collectives  21.9 us (9%)
  matrix products  20.8 us (9%)
  between operations  13.4 us (6%)
  local copies, waits for them, and re-layouts  9.56 us (4%)
    reduce_scatter x1, waiting for transfers between devices, per_device(): lax.psum_scatter(jnp.dot(flat_values, out_proj, preferred_element_type=jn...  99.8 us
    all_gather x1, waiting for transfers between devices, per_device(): all_up = lax.all_gather(value_up, 'dp', axis=0, tiled=True)  43.6 us
    pallas_call x1, Pallas kernels, attend(): pl.pallas_call(functools.partial(attend_kernel, rows_blk, key_blk, halves...  23.4 us
    all_to_all x1, blocking collectives, per_device(): lax.all_to_all(head_values, 'dp', split_axis=1, concat_axis=0, tiled=True)  21.9 us
    dot_general x1, matrix products, per_device(): jnp.dot(flat_values, out_proj, preferred_element_type=jnp.float32)  11 us
    dot_general x1, matrix products, per_device(): jnp.einsum('nhc,hcv->nhv', context, all_up, preferred_element_type=jnp.fl...  9.73 us
    unnamed x16, local copies, waits for them, and re-layouts  6.62 us
  transfers between devices with their start and end apart: 2, of which 2 were waited for; matrix products, arithmetic and copies ran while one was open for 1% of the time, Pallas kernels for 10%

profile of v1, /device:TPU:0, one launch (start us, length us, event | category | flops | bytes accessed | tf_op | source)
XLA Modules:
  0.0 233.2 jit_solution(7415298657333796381)
XLA Ops:
  6.5 0.0 all-gather.2.cloned.1.call-start
  6.5 0.7 all-gather.2.cloned.1.call-update
  7.3 0.0 reduce-scatter.2.cloned.1.call-start
  7.3 2.1 reshape.10.qr_ref
  9.4 0.0 copy-start.1
  9.4 1.0 copy-done.1
  10.4 0.0 copy-start.2
  10.4 0.8 copy-done.2
  11.3 0.0 copy-start.3
  11.3 0.8 copy-done.3
  12.0 0.0 copy-start.4
  12.0 0.7 copy-done.4
  12.7 0.0 copy-start.5
  12.7 0.7 copy-done.5
  13.4 0.0 copy-start.6
  13.4 0.7 copy-done.6
  14.0 23.4 %shard_map.109 = bf16[2,32,64,512]{3,2,1,0:T(8,128)(2,1)S(1)} custom-call(s32[2]{0:T(128)S(1)} %copy-done.5, s32[2]{0:T(128)S(1)} %copy-done.6, bf16[2,32,64,512]{3,2,1,0:T(8,128)(2,1)} %q_ref.1, bf16[2,2048,64]{2,1,0:T(8,128)(2,1)S(1)} %reshape.10.qr_ref, bf16[2,2048,512]{2,1,0:T(8,128)(2,1)} %lat_ref.1, bf16[2,64,2048]{2,1,0:T(8,128)(2,1)S(1)} %copy-done.1, ...), custom_call_target="tpu_custom_call" | custom-call | flops 12999999488 | bytes 14680064 | tf_op jit(solution)/shard_map/pallas_call | solution.py:139
  37.4 0.0 copy-start
  37.4 2.0 copy-done
  39.4 43.6 %all-gather.2.cloned.1.call-done = bf16[64,512,128]{2,1,0:T(8,128)(2,1)} async-done(((bf16[4,512,128]{2,1,0:T(8,128)(2,1)}), bf16[64,512,128]{2,1,0:T(8,128)(2,1)}) %all-gather.2.cloned.1.call-update) | async-done | bytes 8388624 | tf_op jit(solution)/shard_map/all_gather | solution.py:160
  83.0 0.0 copy-start.7
  83.0 9.7 %fusion.5 = bf16[64,64,128]{2,0,1:T(8,128)(2,1)S(1)} fusion(bf16[64,512,128]{2,1,0:T(8,128)(2,1)} %all-gather.2.cloned.1.call-done, bf16[64,64,512]{2,1,0:T(8,128)(2,1)} %bitcast.12), kind=kOutput, calls=%fused_computation.4 | convolution fusion | flops 537395200 | bytes 13631488 | tf_op jit(solution)/shard_map/nhc,hcv->nhv/dot_general | solution.py:164
  92.7 21.9 %all_to_all.15 = bf16[64,64,128]{2,0,1:T(8,128)(2,1)S(1)} all-to-all(bf16[64,64,128]{2,0,1:T(8,128)(2,1)S(1)} %fusion.5), channel_id=1, replica_groups=mesh['grp'=8,'dp'=16] {'dp'}, dimensions={1} | all-to-all | bytes 2097152 | tf_op jit(solution)/shard_map/all_to_all | solution.py:165
  114.6 0.9 copy.16
  115.5 0.0 copy-done.7
  115.5 11.0 %convolution_convert_fusion = bf16[1024,7168]{1,0:T(8,128)(2,1)} fusion(bf16[512,7168]{1,0:T(8,128)(2,1)S(1)} %copy-done.7, bf16[128,8,4,128]{3,2,1,0:T(4,128)(2,1)S(1)} %bitcast.14), kind=kOutput, calls=%fused_computation | convolution fusion | flops 7523532800 | bytes 23068672 | tf_op jit(solution)/shard_map/dot_general | solution.py:168
  126.6 0.0 reduce-scatter.2.cloned.1.call-update
  126.6 99.8 %reduce-scatter.2.cloned.1.call-done = bf16[64,7168]{1,0:T(8,128)(2,1)} async-done(((bf16[1024,7168]{1,0:T(8,128)(2,1)}), bf16[64,7168]{1,0:T(8,128)(2,1)}) %reduce-scatter.2.cloned.1.call-update) | async-done | bytes 917520 | tf_op jit(solution)/shard_map/reduce_scatter | solution.py:167
Async XLA Ops:
  6.5 76.5 %all-gather.2.cloned.1.call-start = ((), (), s32[]{:S(2)}) async-start(), calls=%async_computation.2 | async-start | bytes 8912896 | tf_op jit(solution)/shard_map/all_gather | solution.py:160
  7.3 219.1 %reduce-scatter.2.cloned.1.call-start = ((), (), s32[]{:S(2)}) async-start(), calls=%async_computation.3 | async-start | bytes 15597568 | tf_op jit(solution)/shard_map/reduce_scatter | solution.py:167
  9.4 1.0 copy-start.1
  10.4 0.8 copy-start.2
  11.3 0.8 copy-start.3
  12.0 0.7 copy-start.4
  12.7 0.7 copy-start.5
  13.4 0.7 copy-start.6
  37.4 2.0 copy-start
  83.0 32.5 %copy-start.7 = (bf16[512,7168]{1,0:T(8,128)(2,1)S(1)}, bf16[512,7168]{1,0:T(8,128)(2,1)}, u32[]{:S(2)}) copy-start(bf16[512,7168]{1,0:T(8,128)(2,1)} %param.21) | copy-start | bytes 22020100
Sparse Core Ops, SparseCore 0:
  9.5 73.4 all-gather.1
  126.7 99.5 reduce-scatter.1

commit v2 on v1

v2 whole, which is shorter than its diff:
```python
import functools
import jax
import jax.numpy as jnp
from jax import lax
from jax.experimental import pallas as pl
from jax.experimental.pallas import tpu as pltpu
from jax.sharding import PartitionSpec as P

score_scale = 192.0 ** (-0.5)
log2_e = 1.4426950408889634
very_negative = -1e30
MESH = pl.DeviceIdType.MESH
nt = (((1,), (1,)), ((), ()))


def nbr(base, step):
    return lax.rem(base + step % 4, 4) if step % 4 else base


class Remote:
    def __init__(self, mover, src, dst, step):
        self.mover, self.src, self.dst, self.step = mover, src, dst, step
        self.number = mover.used
        mover.used += 1
        mover.made.append(self)

    def copy(self):
        m = self.mover
        return pltpu.make_async_remote_copy(
            src_ref=self.src(), dst_ref=self.dst(), send_sem=m.send.at[self.number], recv_sem=m.recv.at[self.number],
            device_id=m.device(**self.step), device_id_type=MESH)

    def start(self):
        self.copy().start()
        return self

    def wait_recv(self):
        self.copy().wait_recv()

    def wait_send(self):
        self.copy().wait_send()


class Mover:
    def __init__(self, send, recv):
        self.send, self.recv, self.used, self.made = send, recv, 0, []
        grp, dp = lax.axis_index("grp"), lax.axis_index("dp")
        self.y, self.c = grp // 2, lax.rem(grp, 2)
        self.x, self.z = dp // 4, lax.rem(dp, 4)

    def device(self, x=0, y=0, z=0, c=0):
        cc = lax.rem(self.c + c, 2) if c else self.c
        return (nbr(self.y, y) * 2 + cc, nbr(self.x, x) * 4 + nbr(self.z, z))

    def greet(self, steps):
        barrier = pltpu.get_barrier_semaphore()
        for step in steps:
            pl.semaphore_signal(barrier, inc=1, device_id=self.device(**step), device_id_type=MESH)
        pl.semaphore_wait(barrier, len(steps))

    def later(self, src, dst, **step):
        return Remote(self, src, dst, step)

    def go(self, src, dst, **step):
        return Remote(self, lambda: src, lambda: dst, step).start()


def gather_plan(m, up_ref, proj_ref, all_ref, blk_ref, up_own, blk_own, local):
    x, y, z, c = m.x, m.y, m.z, m.c
    shard = x * 4 + z
    half = pl.ds(pl.multiple_of(c * 256, 256), 256)
    pq = [pl.ds(pl.multiple_of(c * 256 + i * 128, 128), 128) for i in range(2)]
    column = lambda base: pl.ds(base * 4, 4)
    lower = lambda base: pl.ds(base * 4, 2)
    upper = lambda base: pl.ds(base * 4 + 2, 2)
    xl, xr, xo = nbr(x, -1), nbr(x, 1), nbr(x, 2)
    yl, yr, yo = nbr(y, -1), nbr(y, 1), nbr(y, 2)
    zl, zr, zo = nbr(z, -1), nbr(z, 1), nbr(z, 2)

    def at(ref, *index):
        return lambda: ref.at[index]

    def same(ref, *index, **step):
        view = at(ref, *index)
        return m.later(view, view, **step)

    def cols(h):
        return pl.ds(pl.multiple_of(y * 1792 + h * 896, 128), 896)

    def bounce(i, src, mid, dst):
        return (lambda: pltpu.make_async_copy(src(), mid(), local.at[2 * i]),
                lambda: pltpu.make_async_copy(mid(), dst(), local.at[2 * i + 1]))

    own = [bounce(0, at(up_ref, y, half), lambda: up_own, at(all_ref, shard, y, half))]
    for h in range(2):
        own.append(bounce(1 + h, at(proj_ref, slice(None), cols(h)), at(blk_own, h), at(blk_ref, h, z)))

    twins = {}

    def twin(name, ref, *index):
        twins.setdefault(name, []).append(same(ref, *index, c=1))

    zs = [m.later(at(up_ref, y, half), at(all_ref, shard, y, half), z=s) for s in (1, -1, 2)]
    mine = at(proj_ref, slice(None), pl.ds(pl.multiple_of(y * 1792 + c * 896, 128), 896))
    w = [m.later(mine, at(blk_ref, c, z), z=s) for s in (1, -1)]
    wf = [same(blk_ref, c, zl, pl.ds(0, 256), z=1), same(blk_ref, c, zr, pl.ds(256, 256), z=-1)]
    xp = [same(all_ref, column(x), y, pq[0], x=s) for s in (1, -1)]
    yq = [same(all_ref, column(x), y, pq[1], y=s) for s in (1, -1)]
    xpf = [same(all_ref, lower(xl), y, pq[0], x=1), same(all_ref, upper(xr), y, pq[0], x=-1)]
    yqf = [same(all_ref, lower(x), yl, pq[1], y=1), same(all_ref, upper(x), yr, pq[1], y=-1)]
    bases_x, bases_y = (x, xl, xr, xo), (y, yl, yr, yo)
    yp = [[same(all_ref, column(b), y, pq[0], y=s) for s in (1, -1)] for b in bases_x]
    xq = [[same(all_ref, column(x), b, pq[1], x=s) for s in (1, -1)] for b in bases_y]
    ypf = [[same(all_ref, lower(b), yl, pq[0], y=1), same(all_ref, upper(b), yr, pq[0], y=-1)] for b in bases_x]
    xqf = [[same(all_ref, lower(xl), b, pq[1], x=1), same(all_ref, upper(xr), b, pq[1], x=-1)] for b in bases_y]

    twin("spread", all_ref, column(x), y, half)
    for b in (xl, xr):
        twin("near", all_ref, column(b), y, pq[0])
    for b in (yl, yr):
        twin("near", all_ref, column(x), b, pq[1])
    twin("far", all_ref, column(xo), y, pq[0])
    twin("far", all_ref, column(x), yo, pq[1])
    for k in range(4):
        name = "pass%d" % min(k + 1, 3)
        for b in (yl, yr):
            twin(name, all_ref, column(bases_x[k]), b, pq[0])
        for b in (xl, xr):
            twin(name, all_ref, column(b), bases_y[k], pq[1])
        name = "tail%d" % (k // 2)
        twin(name, all_ref, column(bases_x[k]), yo, pq[0])
        twin(name, all_ref, column(xo), bases_y[k], pq[1])
    twin("weights", blk_ref, c, zl)
    twin("weights", blk_ref, c, zr)
    twin("last", blk_ref, c, zo)

    def start(*copies):
        for copy in copies:
            copy.start()

    def got(*copies):
        for copy in copies:
            copy.wait_recv()

    def first():
        for load, _ in own:
            load().start()
        m.greet([dict(x=1), dict(x=-1), dict(y=1), dict(y=-1), dict(z=1), dict(z=-1), dict(z=2), dict(c=1)])
        start(*zs, *w)
        own[0][0]().wait()
        own[0][1]().start()

    def spread():
        for load, store in own[1:]:
            load().wait()
            store().start()
        own[0][1]().wait()
        got(*zs)
        start(*xp, *yq, *yp[0], *xq[0])
        start(*twins["spread"])

    def near():
        got(*xp)
        start(*xpf)
        got(*yq)
        start(*yqf)
        start(*yp[1], *xq[1])
        start(*twins["near"])

    def far():
        got(*xpf, *yqf)
        got(*yp[0], *xq[0])
        start(*yp[2], *xq[2], *ypf[0], *xqf[0])
        start(*twins["far"])

    def pass_on(k):
        def step():
            got(*yp[k], *xq[k])
            start(*ypf[k], *xqf[k])
            if k == 1:
                start(*yp[3], *xq[3])
            start(*twins["pass%d" % k])
        return step

    def weights():
        got(*w)
        start(*wf)
        start(*twins["weights"])

    def tail(name, ks):
        def step():
            for k in ks:
                got(*ypf[k], *xqf[k])
            start(*twins[name])
        return step

    def last():
        got(*wf)
        start(*twins["last"])
        for group in twins.values():
            got(*group)
        for copy in m.made:
            copy.wait_send()
        for _, store in own[1:]:
            store().wait()

    return dict(first=first, spread=spread, near=near, far=far, pass1=pass_on(1), pass2=pass_on(2), pass3=pass_on(3),
                weights=weights, tail0=tail("tail0", (0, 1)), tail1=tail("tail1", (2, 3)), last=last)


schedule = {0: "spread", 3: "near", 5: "far", 7: "pass1", 9: "pass2", 10: "weights", 11: "pass3", 12: "tail0", 13: "tail1"}


def lane_sum(w):
    parts = [w[:, c * 128:(c + 1) * 128] for c in range(w.shape[1] // 128)]
    while len(parts) > 1:
        parts = [a + b for a, b in zip(parts[::2], parts[1::2])] + (parts[-1:] if len(parts) % 2 else [])
    return parts[0]


def attend_kernel(
    len_ref, live_ref, q_hbm, qr_hbm, lat_hbm, rope_hbm, new_ref, newr_ref, anc_ref, up_ref, proj_ref,
    ctx_hbm, all_ref, blk_ref,
    q_ref, qr_ref, lat_ref, rope_ref, up_own, blk_own, top_s, tot_s, acc_s, turn_s, ctx_s,
    send, recv, local, loads,
):
    factor = score_scale * log2_e
    heads, width, key_blk, sub = 64, 512, 1024, 256
    m = Mover(send, recv)
    plan = gather_plan(m, up_ref, proj_ref, all_ref, blk_ref, up_own, blk_own, local)

    def fetch(r):
        pairs = ((q_hbm.at[r], q_ref.at[r]), (qr_hbm.at[r], qr_ref.at[r]), (lat_hbm.at[r], lat_ref.at[r]),
                 (rope_hbm.at[r], rope_ref.at[r, pl.ds(0, 64)]))
        return [pltpu.make_async_copy(src, dst, loads.at[r * 4 + i]) for i, (src, dst) in enumerate(pairs)]

    def deliver(r):
        rows = pl.ds(r * 32, 32)
        return pltpu.make_async_copy(ctx_s.at[:, rows], ctx_hbm.at[:, rows], loads.at[8 + r])

    for r in range(2):
        for copy in fetch(r):
            copy.start()
    plan["first"]()
    for r in range(2):
        position = lax.broadcasted_iota(jnp.int32, (64, 2048), 1)
        row = lax.broadcasted_iota(jnp.int32, (64, 2048), 0)
        outside = jnp.logical_and(row == 0, position >= len_ref[r])
        rope_ref[r, pl.ds(64, 64), :] = jnp.where(outside, very_negative, 0.0).astype(jnp.bfloat16)

    def step(i, carry):
        for r in range(2):
            @pl.when(i == r * 8)
            def _():
                for copy in fetch(r):
                    copy.wait()

        request = i // 8
        block = lax.rem(i, 8) // 2
        key = lax.rem(i, 2)
        row0 = block * 8

        def queries(part):
            start = pl.multiple_of(row0 * heads + part * sub, sub)
            return q_ref[request, pl.ds(start, sub), :], qr_ref[request, pl.ds(start, sub), :]

        @pl.when(key == 0)
        def _():
            for part in range(2):
                q, qr = queries(part)
                rows = pl.ds(part * sub, sub)
                s = lax.dot_general(q, new_ref[request], nt, preferred_element_type=jnp.float32)
                s = s + lax.dot_general(qr[:, :64], newr_ref[request], nt, preferred_element_type=jnp.float32)
                s = s * factor
                anc = anc_ref[request, pl.ds(row0 + part * 4, 4), :]
                bias = jnp.where(anc > 0, 0.0, very_negative)
                s = (s.reshape(4, heads, 32) + bias[:, None, :]).reshape(sub, 32)
                top = jnp.max(s, axis=1, keepdims=True)
                w = jnp.exp2(s - top)
                top_s[rows, :] = jnp.broadcast_to(top, (sub, 128))
                tot_s[rows, :] = jnp.where(lax.broadcasted_iota(jnp.int32, (sub, 128), 1) == 0,
                                           jnp.sum(w, axis=1, keepdims=True), 0.0)
                acc_s[rows, :] = jnp.dot(w.astype(jnp.bfloat16), new_ref[request], preferred_element_type=jnp.float32)

        offset = pl.multiple_of(key * key_blk, key_blk)
        keys = lat_ref[request, pl.ds(offset, key_blk), :]
        rope_keys = rope_ref[request, :, pl.ds(offset, key_blk)]
        scores = []
        for part in range(2):
            q, qr = queries(part)
            scores.append(lax.dot_general(q, keys, nt, preferred_element_type=jnp.float32)
                          + jnp.dot(qr, rope_keys, preferred_element_type=jnp.float32))
        for part in range(2):
            s = scores[part]
            rows = pl.ds(part * sub, sub)
            old = top_s[rows, :]
            new = jnp.maximum(old, jnp.max(s, axis=1, keepdims=True) * factor)
            rescale = jnp.exp2(old - new)
            w = jnp.exp2(s * factor - new[:, :1])
            tot_s[rows, :] = tot_s[rows, :] * rescale + lane_sum(w)
            top_s[rows, :] = new
            acc_s[rows, :] = acc_s[rows, :] * rescale[:, :1] + jnp.dot(
                w.astype(jnp.bfloat16), keys, preferred_element_type=jnp.float32)

        @pl.when(key == 1)
        def _():
            total = jnp.sum(tot_s[...], axis=1, keepdims=True)
            ctx = (acc_s[...] * (1.0 / total)).reshape(8, heads, width)
            alive = row0 + lax.broadcasted_iota(jnp.int32, (8, heads, 1), 0) < live_ref[request]
            ctx = jnp.where(alive, ctx, 0.0)
            turn_s[:, pl.ds(pl.multiple_of(row0, 8), 8), :] = jnp.swapaxes(ctx, 0, 1)

        for r in range(2):
            @pl.when(i == r * 8 + 7)
            def _():
                ctx_s[:, pl.ds(r * 32, 32), :] = turn_s[...].astype(jnp.bfloat16)
                deliver(r).start()

        for point, name in schedule.items():
            pl.when(i == point)(functools.partial(plan[name]))
        return carry

    lax.fori_loop(0, 16, step, 0)
    plan["last"]()
    for r in range(2):
        deliver(r).wait()


def attend(query_lat, query_rope, lat_cache, rope_cache, new_lat, new_rope, cache_len, live_rows, ancestors,
           value_up, out_proj):
    bf = jnp.bfloat16
    queries = query_lat.reshape(2, 2048, 512)
    ropes = query_rope.reshape(2, 2048, 64)
    ropes = jnp.concatenate([ropes, jnp.ones((2, 2048, 1), bf), jnp.zeros((2, 2048, 63), bf)], axis=2)
    anywhere = pl.BlockSpec(memory_space=pl.ANY)
    smem, vmem = pl.BlockSpec(memory_space=pltpu.SMEM), pl.BlockSpec(memory_space=pltpu.VMEM)
    copies = 96
    return pl.pallas_call(
        attend_kernel,
        out_shape=(
            jax.ShapeDtypeStruct((64, 64, 512), bf),
            jax.ShapeDtypeStruct((16,) + value_up.shape, bf),
            jax.ShapeDtypeStruct((2, 4, 512, 896), bf),
        ),
        in_specs=[smem, smem] + [anywhere] * 4 + [vmem] * 3 + [anywhere] * 2,
        out_specs=[anywhere] * 3,
        scratch_shapes=[
            pltpu.VMEM((2, 2048, 512), bf),
            pltpu.VMEM((2, 2048, 128), bf),
            pltpu.VMEM((2, 2048, 512), bf),
            pltpu.VMEM((2, 128, 2048), bf),
            pltpu.VMEM((256, 128), bf),
            pltpu.VMEM((2, 512, 896), bf),
            pltpu.VMEM((512, 128), jnp.float32),
            pltpu.VMEM((512, 128), jnp.float32),
            pltpu.VMEM((512, 512), jnp.float32),
            pltpu.VMEM((64, 32, 512), jnp.float32),
            pltpu.VMEM((64, 64, 512), bf),
            pltpu.SemaphoreType.DMA((copies,)), pltpu.SemaphoreType.DMA((copies,)),
            pltpu.SemaphoreType.DMA((6,)), pltpu.SemaphoreType.DMA((10,)),
        ],
        compiler_params=pltpu.CompilerParams(collective_id=0, has_side_effects=True, vmem_limit_bytes=58 * 2**20),
        cost_estimate=pl.CostEstimate(flops=18 * 10**9, bytes_accessed=40 * 2**20, transcendentals=8 * 2**20),
    )(cache_len, live_rows, queries, ropes, lat_cache, rope_cache, new_lat, new_rope, ancestors, value_up, out_proj)


def project_kernel(
    ctx_hbm, up_hbm, blk_hbm, out_hbm,
    ctx, up, blk, hv, act, part, relay, sums, near, fin, got, send, recv, local,
):
    m = Mover(send, recv)
    x, y = m.x, m.y
    loads = {}
    def load(name, src, dst):
        copy = pltpu.make_async_copy(src, dst, local.at[len(loads)])
        copy.start()
        loads[name] = copy
    load("ctx", ctx_hbm, ctx)
    for dx in (0, 1, 3, 2):
        kb = nbr(x, dx)
        load(dx, up_hbm.at[kb], up.at[dx])
    load("blk", blk_hbm, blk)
    m.greet([dict(x=1), dict(x=-1), dict(x=2), dict(y=1), dict(y=-1), dict(y=2)])

    sent = []

    def go(src, dst, **step):
        copy = m.go(src, dst, **step)
        sent.append(copy)
        return copy

    def values(dx, target):
        kb = nbr(x, dx)
        loads[dx].wait()

        def heads(i, carry):
            h = kb * 16 + i
            v = jnp.dot(ctx[h], up[dx, i], preferred_element_type=jnp.float32)
            target[:, pl.ds(pl.multiple_of(i * 128, 128), 128)] = v.astype(jnp.bfloat16)
            return carry

        lax.fori_loop(0, 16, heads, 0, unroll=4)

    loads["ctx"].wait()
    came = {}
    values(0, act.at[0, 0])
    ys = {(0, 1): go(act.at[0, 0], act.at[3, 0], y=1), (0, 3): go(act.at[0, 0], act.at[1, 0], y=-1)}
    for dx in (1, 3, 2):
        values(dx, hv.at[dx])
        came[-dx % 4] = go(hv.at[dx], act.at[0, -dx % 4], x=dx)
    loads["blk"].wait()

    def product(yr, xr):
        def columns(h, carry):
            part[yr, xr, h] = jnp.dot(act[yr, xr], blk[h], preferred_element_type=jnp.float32).astype(jnp.bfloat16)
            return carry

        lax.fori_loop(0, 2, columns, 0)

    def spread(xr):
        ys[(xr, 1)] = go(act.at[0, xr], act.at[3, xr], y=1)
        ys[(xr, 3)] = go(act.at[0, xr], act.at[1, xr], y=-1)

    far, direct, summed = {}, {}, {}

    def send_far(yr):
        far[(yr, 0)] = go(part.at[yr, 2, 0], relay.at[yr, 0], x=1)
        far[(yr, 1)] = go(part.at[yr, 2, 1], relay.at[yr, 1], x=-1)

    def send_direct(yr, xr):
        if xr == 1:
            direct[(yr, 1)] = go(part.at[yr, 1, 1], near.at[yr, 0, 1], x=1)
        else:
            direct[(yr, 3)] = go(part.at[yr, 3, 0], near.at[yr, 1, 0], x=-1)

    def add(a, b):
        return a.astype(jnp.float32) + b.astype(jnp.float32)

    def send_sum(yr, side):
        far[(yr, side)].wait_recv()
        xr = 1 if side == 0 else 3
        sums[yr, side] = add(part[yr, xr, side], relay[yr, side]).astype(jnp.bfloat16)
        summed[(yr, side)] = go(sums.at[yr, side], near.at[yr, side, side], x=1 if side == 0 else -1)

    out_copies = []

    def write(yr):
        cb = nbr(y, yr)
        for h in range(2):
            cols = pl.ds(pl.multiple_of(cb * 1792 + h * 896, 128), 896)
            copy = pltpu.make_async_copy(got.at[yr, h], out_hbm.at[:, cols], local.at[6 + yr * 2 + h])
            copy.start()
            out_copies.append(copy)

    home = {}

    def finish(yr):
        direct[(yr, 1)].wait_recv()
        direct[(yr, 3)].wait_recv()
        summed[(yr, 0)].wait_recv()
        summed[(yr, 1)].wait_recv()
        for h in range(2):
            total = (add(part[yr, 0, h], near[yr, 0, h]) + near[yr, 1, h].astype(jnp.float32)).astype(jnp.bfloat16)
            if yr:
                fin[yr, h] = total
            else:
                got[0, h] = total
        if yr:
            home[-yr % 4] = go(fin.at[yr], got.at[-yr % 4], y=yr)
        else:
            write(0)

    def arrived(yr, xr):
        if yr == 3:
            ys[(xr, 1)].wait_recv()
        elif yr == 1:
            ys[(xr, 3)].wait_recv()
        else:
            ys[(xr, 2)].wait_recv()

    def forward(xr):
        if xr < 2:
            ys[(xr, 2)] = go(act.at[3, xr], act.at[2, xr], y=1)
        else:
            ys[(xr, 2)] = go(act.at[1, xr], act.at[2, xr], y=-1)

    product(0, 0)
    came[1].wait_recv()
    spread(1)
    product(0, 1)
    came[3].wait_recv()
    product(0, 3)
    for yr in (3, 1):
        arrived(yr, 0)
        product(yr, 0)
    came[2].wait_recv()
    spread(2)
    spread(3)
    product(0, 2)
    send_far(0)
    send_direct(0, 1)
    send_direct(0, 3)
    for yr in (3, 1):
        arrived(yr, 1)
        product(yr, 1)
    send_sum(0, 0)
    send_sum(0, 1)
    send_direct(3, 1)
    send_direct(1, 1)
    arrived(1, 2)
    forward(2)
    forward(0)
    product(1, 2)
    send_far(1)
    arrived(3, 2)
    product(3, 2)
    send_far(3)
    finish(0)
    arrived(1, 3)
    forward(3)
    forward(1)
    product(1, 3)
    send_direct(1, 3)
    arrived(3, 3)
    product(3, 3)
    send_direct(3, 3)
    for yr in (1, 3):
        send_sum(yr, 0)
        send_sum(yr, 1)
    arrived(2, 2)
    product(2, 2)
    send_far(2)
    arrived(2, 0)
    product(2, 0)
    finish(1)
    finish(3)
    arrived(2, 3)
    product(2, 3)
    send_direct(2, 3)
    arrived(2, 1)
    product(2, 1)
    send_direct(2, 1)
    send_sum(2, 0)
    send_sum(2, 1)
    finish(2)
    for yr in (1, 3, 2):
        home[yr].wait_recv()
        write(yr)
    for copy in sent:
        copy.wait_send()
    for copy in out_copies:
        copy.wait()


def project(context, all_up, block):
    bf = jnp.bfloat16
    copies = 48
    return pl.pallas_call(
        project_kernel,
        out_shape=jax.ShapeDtypeStruct((64, 7168), bf),
        in_specs=[pl.BlockSpec(memory_space=pl.ANY)] * 3,
        out_specs=pl.BlockSpec(memory_space=pl.ANY),
        scratch_shapes=[
            pltpu.VMEM((64, 64, 512), bf),
            pltpu.VMEM((4, 16, 512, 128), bf),
            pltpu.VMEM((2, 2048, 896), bf),
            pltpu.VMEM((4, 64, 2048), bf),
            pltpu.VMEM((4, 4, 64, 2048), bf),
            pltpu.VMEM((4, 4, 2, 64, 896), bf),
            pltpu.VMEM((4, 2, 64, 896), bf),
            pltpu.VMEM((4, 2, 64, 896), bf),
            pltpu.VMEM((4, 2, 2, 64, 896), bf),
            pltpu.VMEM((4, 2, 64, 896), bf),
            pltpu.VMEM((4, 2, 64, 896), bf),
            pltpu.SemaphoreType.DMA((copies,)), pltpu.SemaphoreType.DMA((copies,)), pltpu.SemaphoreType.DMA((14,)),
        ],
        compiler_params=pltpu.CompilerParams(collective_id=1, has_side_effects=True, vmem_limit_bytes=56 * 2**20),
        cost_estimate=pl.CostEstimate(flops=8 * 10**9, bytes_accessed=24 * 2**20, transcendentals=0),
    )(context, all_up.reshape(4, 16, 512, 128), block.reshape(2, 2048, 896))


def per_device(query_lat, query_rope, lat_cache, rope_cache, new_lat, new_rope, cache_len, live_rows, ancestors,
               value_up, out_proj):
    context, all_up, block = attend(
        query_lat, query_rope, lat_cache, rope_cache, new_lat, new_rope, cache_len, live_rows, ancestors,
        value_up, out_proj)
    return project(context, all_up, block)


def solution(mesh):
    both = ("grp", "dp")
    in_specs = (
        P(both, None, None, None), P(both, None, None), P(both, None, None), P(both, None, None),
        P(both, None, None), P(both, None, None), P(both), P(both), P(both, None, None),
        P("dp", None, None), P("dp", None),
    )
    return jax.shard_map(per_device, mesh=mesh, in_specs=in_specs, out_specs=P(both, None), check_vma=False)
```

time: 234 us -> 130 us (0.56)
  waiting for transfers between devices: 144 us -> 0 us
  Pallas kernels: 23.4 us -> 124 us
  blocking collectives: 21.9 us -> 0 us
  matrix products: 20.8 us -> 0 us
  between operations: 13.4 us -> 0.03 us
  local copies, waits for them, and re-layouts: 9.56 us -> 4.37 us
    pallas_call x1 -> x2, Pallas kernels: 23.4 us -> 124 us  [the longest x1 69.7 us: project(): pl.pallas_call(project_kernel, out_shape=jax.ShapeDtypeStruct((64, 7168),...]
    reduce_scatter x1 -> x0, waiting for transfers between devices: 99.8 us -> none  [per_device(): lax.psum_scatter(jnp.dot(flat_values, out_proj, preferred_element_type=jn...]
    all_gather x1 -> x0, waiting for transfers between devices: 43.6 us -> none  [per_device(): all_up = lax.all_gather(value_up, 'dp', axis=0, tiled=True)]
    all_to_all x1 -> x0, blocking collectives: 21.9 us -> none  [per_device(): lax.all_to_all(head_values, 'dp', split_axis=1, concat_axis=0, tiled=True)]
    dot_general x2 -> x0, matrix products: 20.8 us -> none  [the longest x1 11 us: per_device(): jnp.dot(flat_values, out_proj, preferred_element_type=jnp.float32)]
    unnamed x16 -> x1, local copies, waits for them, and re-layouts: 6.62 us -> 2.16 us
  transfers between devices with their start and end apart: 2 -> 0, of which waited for: 2 -> 0; matrix products, arithmetic and copies ran while one was open for 1% -> 0% of each run, Pallas kernels for 10% -> 0%
where the time goes in v2:
time: 130 us
  Pallas kernels  124 us (95%)
  local copies, waits for them, and re-layouts  4.37 us (3%)
  other arithmetic  1.33 us (1%)
    pallas_call x1, Pallas kernels, project(): pl.pallas_call(project_kernel, out_shape=jax.ShapeDtypeStruct((64, 7168),...  69.7 us
    pallas_call x1, Pallas kernels, attend(): pl.pallas_call(attend_kernel, out_shape=(jax.ShapeDtypeStruct((64, 64, 51...  54.6 us

profile of v2, /device:TPU:0, one launch (start us, length us, event | category | flops | bytes accessed | tf_op | source)
XLA Modules:
  0.0 129.9 jit_solution(9592481004063081986)
XLA Ops:
  0.0 0.1 pad.1.clone
  0.1 0.1 pad.2.clone
  0.2 2.1 %reshape.13 = bf16[2,2048,64]{2,1,0:T(8,128)(2,1)S(1)} reshape(bf16[2,32,4096]{2,1,0:T(8,128)(2,1)} %param.12) | data formatting | bytes 1048576 | tf_op jit(solution)/shard_map/reshape | solution.py:333
  2.2 1.3 %maximum_maximum_fusion.qr_hbm = bf16[2,2048,128]{2,1,0:T(8,128)(2,1)} fusion(bf16[2,2048,64]{2,1,0:T(8,128)(2,1)S(1)} %reshape.13, bf16[128]{0:T(256)(128)(2,1)S(1)} %pad.2.clone, bf16[128]{0:T(256)(128)(2,1)S(1)} %pad.1.clone), kind=kLoop, calls=%fused_computation | loop fusion | flops 3145728 | bytes 1573376 | tf_op jit(solution)/shard_map/concatenate | solution.py:334
  3.5 54.6 %shard_map.109 = (bf16[64,64,512]{2,1,0:T(8,128)(2,1)}, bf16[16,4,512,128]{3,2,1,0:T(8,128)(2,1)}, bf16[2,4,512,896]{3,2,1,0:T(8,128)(2,1)}) custom-call(s32[2]{0:T(128)} %len_ref.1, s32[2]{0:T(128)} %live_ref.1, bf16[2,2048,512]{2,1,0:T(8,128)(2,1)} %bitcast.4, bf16[2,2048,128]{2,1,0:T(8,128)(2,1)} %maximum_maximum_fusion.qr_hbm, ...), custom_call_target="tpu_custom_call" | custom-call | flops 17999998976 | bytes 41943040 | tf_op jit(solution)/shard_map/pallas_call | solution.py:338
  58.1 69.7 %shard_map.110 = bf16[64,7168]{1,0:T(8,128)(2,1)} custom-call(bf16[64,64,512]{2,1,0:T(8,128)(2,1)} %get-tuple-element.8.ctx_hbm, bf16[4,16,512,128]{3,2,1,0:T(8,128)(2,1)} %bitcast.5, bf16[2,2048,896]{2,1,0:T(8,128)(2,1)} %bitcast.6), custom_call_target="tpu_custom_call" | custom-call | flops 8000000000 | bytes 25165824 | tf_op jit(solution)/shard_map/pallas_call | solution.py:558
  127.8 2.2 %copy.13 = bf16[64,7168]{1,0:T(8,128)(2,1)} copy(bf16[64,7168]{1,0:T(8,128)(2,1)} %shard_map.110) | data formatting | bytes 1835008
  (1 shorter events, 0.0 us)

commit v3 on v2

v3 whole, which is shorter than its diff:
```python
import functools
import jax
import jax.numpy as jnp
from jax import lax
from jax.experimental import pallas as pl
from jax.experimental.pallas import tpu as pltpu
from jax.sharding import PartitionSpec as P

score_scale = 192.0 ** (-0.5)
log2_e = 1.4426950408889634
very_negative = -1e30
MESH = pl.DeviceIdType.MESH
nt = (((1,), (1,)), ((), ()))


def nbr(base, step):
    return lax.rem(base + step % 4, 4) if step % 4 else base


class Remote:
    def __init__(self, mover, src, dst, step):
        self.mover, self.src, self.dst, self.step = mover, src, dst, step
        self.number = mover.used
        mover.used += 1
        mover.made.append(self)

    def copy(self):
        m = self.mover
        return pltpu.make_async_remote_copy(
            src_ref=self.src(), dst_ref=self.dst(), send_sem=m.send.at[self.number], recv_sem=m.recv.at[self.number],
            device_id=m.device(**self.step), device_id_type=MESH)

    def start(self):
        self.copy().start()
        return self

    def wait_recv(self):
        self.copy().wait_recv()

    def wait_send(self):
        self.copy().wait_send()


class Mover:
    def __init__(self, send, recv):
        self.send, self.recv, self.used, self.made = send, recv, 0, []
        grp, dp = lax.axis_index("grp"), lax.axis_index("dp")
        self.y, self.c = grp // 2, lax.rem(grp, 2)
        self.x, self.z = dp // 4, lax.rem(dp, 4)

    def device(self, x=0, y=0, z=0, c=0):
        cc = lax.rem(self.c + c, 2) if c else self.c
        return (nbr(self.y, y) * 2 + cc, nbr(self.x, x) * 4 + nbr(self.z, z))

    def greet(self, steps):
        barrier = pltpu.get_barrier_semaphore()
        for step in steps:
            pl.semaphore_signal(barrier, inc=1, device_id=self.device(**step), device_id_type=MESH)
        pl.semaphore_wait(barrier, len(steps))

    def later(self, src, dst, **step):
        return Remote(self, src, dst, step)

    def go(self, src, dst, **step):
        return Remote(self, lambda: src, lambda: dst, step).start()


def gather_plan(m, up_ref, proj_ref, all_ref, blk_ref, local):
    x, y, z, c = m.x, m.y, m.z, m.c
    shard = x * 4 + z
    half = pl.ds(pl.multiple_of(c * 256, 256), 256)
    pq = [pl.ds(pl.multiple_of(c * 256 + i * 128, 128), 128) for i in range(2)]
    column = lambda base: pl.ds(base * 4, 4)
    lower = lambda base: pl.ds(base * 4, 2)
    upper = lambda base: pl.ds(base * 4 + 2, 2)
    xl, xr, xo = nbr(x, -1), nbr(x, 1), nbr(x, 2)
    yl, yr, yo = nbr(y, -1), nbr(y, 1), nbr(y, 2)
    zl, zr, zo = nbr(z, -1), nbr(z, 1), nbr(z, 2)

    def at(ref, *index):
        return lambda: ref.at[index]

    def same(ref, *index, **step):
        view = at(ref, *index)
        return m.later(view, view, **step)

    def cols(h):
        return pl.ds(pl.multiple_of(y * 1792 + h * 896, 128), 896)

    own = [lambda: pltpu.make_async_copy(up_ref.at[y, half], all_ref.at[shard, y, half], local.at[0])]
    for h in range(2):
        own.append(lambda h=h: pltpu.make_async_copy(proj_ref.at[:, cols(h)], blk_ref.at[h, z], local.at[1 + h]))

    twins = {}

    def twin(name, ref, *index):
        twins.setdefault(name, []).append(same(ref, *index, c=1))

    zs = [m.later(at(up_ref, y, half), at(all_ref, shard, y, half), z=s) for s in (1, -1, 2)]
    mine = at(proj_ref, slice(None), pl.ds(pl.multiple_of(y * 1792 + c * 896, 128), 896))
    w = [m.later(mine, at(blk_ref, c, z), z=s) for s in (1, -1)]
    wf = [same(blk_ref, c, zl, pl.ds(0, 256), z=1), same(blk_ref, c, zr, pl.ds(256, 256), z=-1)]
    xp = [same(all_ref, column(x), y, pq[0], x=s) for s in (1, -1)]
    yq = [same(all_ref, column(x), y, pq[1], y=s) for s in (1, -1)]
    xpf = [same(all_ref, lower(xl), y, pq[0], x=1), same(all_ref, upper(xr), y, pq[0], x=-1)]
    yqf = [same(all_ref, lower(x), yl, pq[1], y=1), same(all_ref, upper(x), yr, pq[1], y=-1)]
    bases_x, bases_y = (x, xl, xr, xo), (y, yl, yr, yo)
    yp = [[same(all_ref, column(b), y, pq[0], y=s) for s in (1, -1)] for b in bases_x]
    xq = [[same(all_ref, column(x), b, pq[1], x=s) for s in (1, -1)] for b in bases_y]
    ypf = [[same(all_ref, lower(b), yl, pq[0], y=1), same(all_ref, upper(b), yr, pq[0], y=-1)] for b in bases_x]
    xqf = [[same(all_ref, lower(xl), b, pq[1], x=1), same(all_ref, upper(xr), b, pq[1], x=-1)] for b in bases_y]

    twin("spread", all_ref, column(x), y, half)
    for b in (xl, xr):
        twin("near", all_ref, column(b), y, pq[0])
    for b in (yl, yr):
        twin("near", all_ref, column(x), b, pq[1])
    twin("far", all_ref, column(xo), y, pq[0])
    twin("far", all_ref, column(x), yo, pq[1])
    for k in range(4):
        name = "pass%d" % min(k + 1, 3)
        for b in (yl, yr):
            twin(name, all_ref, column(bases_x[k]), b, pq[0])
        for b in (xl, xr):
            twin(name, all_ref, column(b), bases_y[k], pq[1])
        name = "tail%d" % (k // 2)
        twin(name, all_ref, column(bases_x[k]), yo, pq[0])
        twin(name, all_ref, column(xo), bases_y[k], pq[1])
    twin("weights", blk_ref, c, zl)
    twin("weights", blk_ref, c, zr)
    twin("last", blk_ref, c, zo)

    def start(*copies):
        for copy in copies:
            copy.start()

    def got(*copies):
        for copy in copies:
            copy.wait_recv()

    def first():
        for load in own:
            load().start()
        m.greet([dict(x=1), dict(x=-1), dict(x=2), dict(y=1), dict(y=-1), dict(y=2),
                 dict(z=1), dict(z=-1), dict(z=2), dict(c=1)])
        start(*zs)

    def spread():
        own[0]().wait()
        got(*zs)
        start(*w)
        start(*xp, *yq, *yp[0], *xq[0])
        start(*twins["spread"])

    def near():
        got(*xp)
        start(*xpf)
        got(*yq)
        start(*yqf)
        start(*yp[1], *xq[1], *yp[2], *xq[2])
        start(*twins["near"])

    def far():
        got(*xpf, *yqf)
        got(*yp[0], *xq[0])
        start(*ypf[0], *xqf[0], *yp[3], *xq[3])
        start(*twins["far"])

    def pass_on(k):
        def step():
            got(*yp[k], *xq[k])
            start(*ypf[k], *xqf[k])
            start(*twins["pass%d" % k])
        return step

    def weights():
        got(*w)
        start(*wf)
        start(*twins["weights"])

    def tail(name, ks):
        def step():
            for k in ks:
                got(*ypf[k], *xqf[k])
            start(*twins[name])
        return step

    def ready():
        for name, group in twins.items():
            if name not in ("weights", "last"):
                got(*group)

    def block_ready():
        got(*wf)
        start(*twins["last"])
        got(*twins["weights"], *twins["last"])
        for load in own[1:]:
            load().wait()

    return dict(first=first, spread=spread, near=near, far=far, pass1=pass_on(1), pass2=pass_on(2), pass3=pass_on(3),
                weights=weights, ready=ready, block_ready=block_ready, tail0=tail("tail0", (0, 1)), tail1=tail("tail1", (2, 3)))


schedule = {
    0: ["spread"], 2: ["near"], 4: ["far"], 5: ["pass1"], 6: ["pass2"], 7: ["pass3"], 8: ["tail0"], 9: ["tail1"],
    11: ["open", "weights"], 13: ["side"], 14: ["across"],
}


def lane_sum(w):
    parts = [w[:, c * 128:(c + 1) * 128] for c in range(w.shape[1] // 128)]
    while len(parts) > 1:
        parts = [a + b for a, b in zip(parts[::2], parts[1::2])] + (parts[-1:] if len(parts) % 2 else [])
    return parts[0]


def add(a, b):
    return a.astype(jnp.float32) + b.astype(jnp.float32)


class Project:
    def __init__(self, m, out_hbm, ctx, up, blk, hv, act, part, relay, sums, near, fin, got, writes):
        self.m, self.out_hbm, self.ctx, self.up, self.blk, self.hv, self.act, self.part = (
            m, out_hbm, ctx, up, blk, hv, act, part)
        self.relay, self.sums, self.near, self.fin, self.got, self.writes = relay, sums, near, fin, got, writes

        def copy(src, i, dst, j, **step):
            return m.later(lambda: src.at[i], lambda: dst.at[j], **step)

        both, four = range(2), range(4)
        self.swap = {(q, dx): copy(hv, (q, dx), act, (q, 0, -dx % 4), x=dx) for q in both for dx in (1, 3, 2)}
        self.wide = {(q, xr, s): copy(act, (q, 0, xr), act, (q, -s % 4, xr), y=s)
                     for q in both for xr in four for s in (1, -1)}
        self.on = {(q, xr): (copy(act, (q, 3, xr), act, (q, 2, xr), y=1) if xr < 2 else
                             copy(act, (q, 1, xr), act, (q, 2, xr), y=-1)) for q in both for xr in four}
        self.far, self.direct, self.summed, self.home = {}, {}, {}, {}
        for q in both:
            for yr in four:
                for side, xr, way in ((0, 1, 1), (1, 3, -1)):
                    k = (q, yr, side)
                    self.far[k] = copy(part, (q, yr, 2, side), relay, (q, yr, side), x=way)
                    self.direct[k] = copy(part, (q, yr, xr, 1 - side), near, (q, yr, side, 1 - side), x=way)
                    self.summed[k] = copy(sums, (q, yr, side), near, (q, yr, side, side), x=way)
                if yr:
                    self.home[q, yr] = copy(fin, (q, yr), got, (q, -yr % 4), y=yr)

    def values(self, q, dx, target):
        kb = nbr(self.m.x, dx)

        def heads(i, carry):
            h = kb * 16 + i
            v = jnp.dot(self.ctx[h], self.up[h // 4, lax.rem(h, 4)], preferred_element_type=jnp.float32)
            target[:, pl.ds(pl.multiple_of(i * 128, 128), 128)] = v.astype(jnp.bfloat16)
            return carry

        lax.fori_loop(0, 16, heads, 0, unroll=4)

    def open(self, q):
        for dx in (1, 3, 2):
            self.values(q, dx, self.hv.at[q, dx])
            self.swap[q, dx].start()
        self.values(q, 0, self.act.at[q, 0, 0])

    def widen(self, q, xr):
        if xr:
            self.swap[q, -xr % 4].wait_recv()
        self.wide[q, xr, 1].start()
        self.wide[q, xr, -1].start()

    def arrived(self, q, yr, xr):
        if yr == 2:
            self.on[q, xr].wait_recv()
        else:
            self.wide[q, xr, 1 if yr == 3 else -1].wait_recv()

    def pass_on(self, q, *xrs):
        for xr in xrs:
            self.arrived(q, 3 if xr < 2 else 1, xr)
            self.on[q, xr].start()

    def rest(self, q):
        for xr in (2, 3):
            self.arrived(q, 3, xr)
        for xr in (0, 1):
            self.arrived(q, 1, xr)

    def product(self, q, yr):
        def columns(h, carry):
            rows = self.act[q, yr].reshape(128, 2048)
            p = jnp.dot(rows, self.blk[h].reshape(2048, 896), preferred_element_type=jnp.float32).astype(jnp.bfloat16)
            for xr in range(4):
                self.part[q, yr, xr, h] = p[xr * 32:(xr + 1) * 32]
            return carry

        lax.fori_loop(0, 2, columns, 0)
        for side in range(2):
            self.far[q, yr, side].start()
        for side in range(2):
            self.direct[q, yr, side].start()

    def pass_sums(self, q, yr):
        for side, xr in ((0, 1), (1, 3)):
            self.far[q, yr, side].wait_recv()
            self.sums[q, yr, side] = add(self.part[q, yr, xr, side], self.relay[q, yr, side]).astype(jnp.bfloat16)
            self.summed[q, yr, side].start()

    def write(self, q, yr):
        cb = nbr(self.m.y, yr)
        copies = []
        for h in range(2):
            cols = pl.ds(pl.multiple_of(cb * 1792 + h * 896, 128), 896)
            copies.append(pltpu.make_async_copy(
                self.got.at[q, yr, h], self.out_hbm.at[pl.ds(q * 32, 32), cols], self.writes.at[q * 8 + yr * 2 + h]))
        return copies

    def finish(self, q, yr):
        for side in range(2):
            self.direct[q, yr, side].wait_recv()
            self.summed[q, yr, side].wait_recv()
        for h in range(2):
            total = (add(self.part[q, yr, 0, h], self.near[q, yr, 0, h])
                     + self.near[q, yr, 1, h].astype(jnp.float32)).astype(jnp.bfloat16)
            if yr:
                self.fin[q, yr, h] = total
            else:
                self.got[q, 0, h] = total
        if yr:
            self.home[q, yr].start()
        else:
            for copy in self.write(q, 0):
                copy.start()


def layer_kernel(
    len_ref, live_ref, q_hbm, qr_hbm, lat_hbm, rope_hbm, new_ref, newr_ref, anc_ref, up_ref, proj_ref,
    out_hbm,
    q_ref, raw_s, qr_ref, lat_ref, rope_ref, top_s, tot_s, acc_s, turn_s, ctx_s, all_ref, blk_ref,
    hv, act, part, relay, sums, near, fin, got,
    send, recv, local, loads, writes,
):
    factor = score_scale * log2_e
    heads, width, key_blk, sub = 64, 512, 1024, 256
    m = Mover(send, recv)
    plan = gather_plan(m, up_ref, proj_ref, all_ref, blk_ref, local)
    project = Project(m, out_hbm, ctx_s, all_ref, blk_ref, hv, act, part, relay, sums, near, fin, got, writes)

    def begin():
        plan["ready"]()
        project.open(0)
        project.widen(0, 0)

    def side():
        project.widen(0, 1)
        project.widen(0, 3)

    plan.update(open=begin, side=side, across=lambda: project.widen(0, 2))

    def fetch_ropes(r):
        return pltpu.make_async_copy(qr_hbm.at[r], raw_s.at[r], loads.at[6 + r])

    def arrange_ropes(r):
        fetch_ropes(r).wait()
        lane = lax.broadcasted_iota(jnp.int32, (32, 128), 1)
        after = jnp.where(lane == 64, 1.0, 0.0)

        def pair(i, carry):
            both = raw_s[r, :, pl.ds(pl.multiple_of(i * 128, 128), 128)].astype(jnp.float32)
            turn_s[2 * i, :, pl.ds(0, 128)] = jnp.where(lane < 64, both, after)
            turn_s[2 * i + 1, :, pl.ds(0, 128)] = jnp.where(lane < 64, pltpu.roll(both, 64, 1), after)
            return carry

        lax.fori_loop(0, heads // 2, pair, 0, unroll=4)
        for block in range(4):
            turned = jnp.swapaxes(turn_s[:, pl.ds(block * 8, 8), pl.ds(0, 128)], 0, 1)
            qr_ref[r, pl.ds(block * 512, 512), :] = turned.reshape(512, 128).astype(jnp.bfloat16)

    def fetch(r):
        pairs = ((q_hbm.at[r], q_ref.at[r]), (lat_hbm.at[r], lat_ref.at[r]),
                 (rope_hbm.at[r], rope_ref.at[r, pl.ds(0, 64)]))
        return [pltpu.make_async_copy(src, dst, loads.at[r * 3 + i]) for i, (src, dst) in enumerate(pairs)]

    for r in range(2):
        for copy in fetch(r):
            copy.start()
        fetch_ropes(r).start()
    plan["first"]()
    for r in range(2):
        position = lax.broadcasted_iota(jnp.int32, (64, 2048), 1)
        row = lax.broadcasted_iota(jnp.int32, (64, 2048), 0)
        outside = jnp.logical_and(row == 0, position >= len_ref[r])
        arrange_ropes(r)
        rope_ref[r, pl.ds(64, 64), :] = jnp.where(outside, very_negative, 0.0).astype(jnp.bfloat16)

    def step(i, carry):
        for r in range(2):
            @pl.when(i == r * 8)
            def _():
                for copy in fetch(r):
                    copy.wait()

        request = i // 8
        block = lax.rem(i, 8) // 2
        key = lax.rem(i, 2)
        row0 = block * 8

        def queries(part):
            start = pl.multiple_of(row0 * heads + part * sub, sub)
            return q_ref[request, pl.ds(start, sub), :], qr_ref[request, pl.ds(start, sub), :]

        @pl.when(key == 0)
        def _():
            for part in range(2):
                q, qr = queries(part)
                rows = pl.ds(part * sub, sub)
                s = lax.dot_general(q, new_ref[request], nt, preferred_element_type=jnp.float32)
                s = s + lax.dot_general(qr[:, :64], newr_ref[request], nt, preferred_element_type=jnp.float32)
                s = s * factor
                anc = anc_ref[request, pl.ds(row0 + part * 4, 4), :]
                bias = jnp.where(anc > 0, 0.0, very_negative)
                s = (s.reshape(4, heads, 32) + bias[:, None, :]).reshape(sub, 32)
                top = jnp.max(s, axis=1, keepdims=True)
                w = jnp.exp2(s - top)
                top_s[rows, :] = jnp.broadcast_to(top, (sub, 128))
                tot_s[rows, :] = jnp.where(lax.broadcasted_iota(jnp.int32, (sub, 128), 1) == 0,
                                           jnp.sum(w, axis=1, keepdims=True), 0.0)
                acc_s[rows, :] = jnp.dot(w.astype(jnp.bfloat16), new_ref[request], preferred_element_type=jnp.float32)

        offset = pl.multiple_of(key * key_blk, key_blk)
        keys = lat_ref[request, pl.ds(offset, key_blk), :]
        rope_keys = rope_ref[request, :, pl.ds(offset, key_blk)]
        scores = []
        for part in range(2):
            q, qr = queries(part)
            scores.append(lax.dot_general(q, keys, nt, preferred_element_type=jnp.float32)
                          + jnp.dot(qr, rope_keys, preferred_element_type=jnp.float32))
        for part in range(2):
            s = scores[part]
            rows = pl.ds(part * sub, sub)
            old = top_s[rows, :]
            new = jnp.maximum(old, jnp.max(s, axis=1, keepdims=True) * factor)
            rescale = jnp.exp2(old - new)
            w = jnp.exp2(s * factor - new[:, :1])
            tot_s[rows, :] = tot_s[rows, :] * rescale + lane_sum(w)
            top_s[rows, :] = new
            acc_s[rows, :] = acc_s[rows, :] * rescale[:, :1] + jnp.dot(
                w.astype(jnp.bfloat16), keys, preferred_element_type=jnp.float32)

        @pl.when(key == 1)
        def _():
            total = jnp.sum(tot_s[...], axis=1, keepdims=True)
            ctx = (acc_s[...] * (1.0 / total)).reshape(8, heads, width)
            alive = row0 + lax.broadcasted_iota(jnp.int32, (8, heads, 1), 0) < live_ref[request]
            ctx = jnp.where(alive, ctx, 0.0)
            turn_s[:, pl.ds(pl.multiple_of(row0, 8), 8), :] = jnp.swapaxes(ctx, 0, 1)

        @pl.when(i == 7)
        def _():
            ctx_s[...] = turn_s[...].astype(jnp.bfloat16)

        for point, names in schedule.items():
            @pl.when(i == point)
            def _():
                for name in names:
                    plan[name]()
        return carry

    lax.fori_loop(0, 16, step, 0)
    ctx_s[...] = turn_s[...].astype(jnp.bfloat16)
    p = project
    p.open(1)
    plan["block_ready"]()
    p.product(0, 0)
    p.pass_on(0, 0, 2)
    p.widen(1, 0)
    p.pass_sums(0, 0)
    p.pass_on(0, 1, 3)
    p.rest(0)
    p.product(0, 3)
    p.product(0, 1)
    p.widen(1, 1)
    p.widen(1, 3)
    p.pass_sums(0, 3)
    p.pass_sums(0, 1)
    p.widen(1, 2)
    p.finish(0, 0)
    for xr in range(4):
        p.arrived(0, 2, xr)
    p.product(0, 2)
    p.product(1, 0)
    p.finish(0, 3)
    p.finish(0, 1)
    p.pass_on(1, 0, 2)
    p.pass_sums(0, 2)
    p.pass_sums(1, 0)
    p.pass_on(1, 1, 3)
    p.rest(1)
    p.product(1, 3)
    p.product(1, 1)
    p.finish(0, 2)
    p.pass_sums(1, 3)
    p.pass_sums(1, 1)
    p.finish(1, 0)
    for xr in range(4):
        p.arrived(1, 2, xr)
    p.product(1, 2)
    p.finish(1, 3)
    p.finish(1, 1)
    p.pass_sums(1, 2)
    p.finish(1, 2)
    for q in range(2):
        for yr in (1, 3, 2):
            p.home[q, -yr % 4].wait_recv()
            for copy in p.write(q, yr):
                copy.start()
    for copy in m.made:
        copy.wait_send()
    for q in range(2):
        for yr in range(4):
            for copy in p.write(q, yr):
                copy.wait()


def layer(query_lat, query_rope, lat_cache, rope_cache, new_lat, new_rope, cache_len, live_rows, ancestors,
           value_up, out_proj):
    bf = jnp.bfloat16
    queries = query_lat.reshape(2, 2048, 512)
    anywhere = pl.BlockSpec(memory_space=pl.ANY)
    smem, vmem = pl.BlockSpec(memory_space=pltpu.SMEM), pl.BlockSpec(memory_space=pltpu.VMEM)
    copies = 176
    return pl.pallas_call(
        layer_kernel,
        out_shape=jax.ShapeDtypeStruct((64, 7168), bf),
        in_specs=[smem, smem] + [anywhere] * 4 + [vmem] * 3 + [anywhere] * 2,
        out_specs=anywhere,
        scratch_shapes=[
            pltpu.VMEM((2, 2048, 512), bf),
            pltpu.VMEM((2, 32, 4096), bf),
            pltpu.VMEM((2, 2048, 128), bf),
            pltpu.VMEM((2, 2048, 512), bf),
            pltpu.VMEM((2, 128, 2048), bf),
            pltpu.VMEM((512, 128), jnp.float32),
            pltpu.VMEM((512, 128), jnp.float32),
            pltpu.VMEM((512, 512), jnp.float32),
            pltpu.VMEM((64, 32, 512), jnp.float32),
            pltpu.VMEM((64, 32, 512), bf),
            pltpu.VMEM((16, 4, 512, 128), bf),
            pltpu.VMEM((2, 4, 512, 896), bf),
            pltpu.VMEM((2, 4, 32, 2048), bf),
            pltpu.VMEM((2, 4, 4, 32, 2048), bf),
            pltpu.VMEM((2, 4, 4, 2, 32, 896), bf),
            pltpu.VMEM((2, 4, 2, 32, 896), bf),
            pltpu.VMEM((2, 4, 2, 32, 896), bf),
            pltpu.VMEM((2, 4, 2, 2, 32, 896), bf),
            pltpu.VMEM((2, 4, 2, 32, 896), bf),
            pltpu.VMEM((2, 4, 2, 32, 896), bf),
            pltpu.SemaphoreType.DMA((copies,)), pltpu.SemaphoreType.DMA((copies,)),
            pltpu.SemaphoreType.DMA((3,)), pltpu.SemaphoreType.DMA((8,)), pltpu.SemaphoreType.DMA((16,)),
        ],
        compiler_params=pltpu.CompilerParams(collective_id=0, has_side_effects=True, vmem_limit_bytes=62 * 2**20),
        cost_estimate=pl.CostEstimate(flops=26 * 10**9, bytes_accessed=40 * 2**20, transcendentals=8 * 2**20),
    )(cache_len, live_rows, queries, query_rope, lat_cache, rope_cache, new_lat, new_rope, ancestors, value_up, out_proj)


def per_device(query_lat, query_rope, lat_cache, rope_cache, new_lat, new_rope, cache_len, live_rows, ancestors,
               value_up, out_proj):
    return layer(query_lat, query_rope, lat_cache, rope_cache, new_lat, new_rope, cache_len, live_rows, ancestors,
                 value_up, out_proj)


def solution(mesh):
    both = ("grp", "dp")
    in_specs = (
        P(both, None, None, None), P(both, None, None), P(both, None, None), P(both, None, None),
        P(both, None, None), P(both, None, None), P(both), P(both), P(both, None, None),
        P("dp", None, None), P("dp", None),
    )
    return jax.shard_map(per_device, mesh=mesh, in_specs=in_specs, out_specs=P(both, None), check_vma=False)
```

time: 130 us -> 109 us (0.84)
  Pallas kernels: 124 us -> 106 us
  local copies, waits for them, and re-layouts: 4.37 us -> 2.16 us
  other arithmetic: 1.33 us -> 0 us
    pallas_call x2 -> x1, Pallas kernels: 124 us -> 106 us  [layer(): pl.pallas_call(layer_kernel, out_shape=jax.ShapeDtypeStruct((64, 7168), b...]
    reshape x1 -> x0, local copies, waits for them, and re-layouts: 2.05 us -> none  [attend(): ropes = query_rope.reshape(2, 2048, 64)]
    concatenate x1 -> x0, other arithmetic: 1.33 us -> none  [attend(): jnp.concatenate([ropes, jnp.ones((2, 2048, 1), bf), jnp.zeros((2, 2048, 6...]
where the time goes in v3:
time: 109 us; the launch traced here: 108 us
  Pallas kernels  106 us (97%)
  local copies, waits for them, and re-layouts  2.16 us (2%)
    pallas_call x1, Pallas kernels, layer(): pl.pallas_call(layer_kernel, out_shape=jax.ShapeDtypeStruct((64, 7168), b...  106 us

profile of v3, /device:TPU:0, one launch (start us, length us, event | category | flops | bytes accessed | tf_op | source)
XLA Modules:
  0.0 107.8 jit_solution(18242275309183073087)
XLA Ops:
  0.0 105.7 %shard_map.109 = bf16[64,7168]{1,0:T(8,128)(2,1)} custom-call(s32[2]{0:T(128)} %len_ref.1, s32[2]{0:T(128)} %live_ref.1, bf16[2,2048,512]{2,1,0:T(8,128)(2,1)} %bitcast.1, bf16[2,32,4096]{2,1,0:T(8,128)(2,1)} %qr_hbm.1, bf16[2,2048,512]{2,1,0:T(8,128)(2,1)} %lat_hbm.1, bf16[2,64,2048]{2,1,0:T(8,128)(2,1)} %rope_hbm.1, bf16[2,32,512]{2,1,0:T(8,128)(2,1)} %new_ref.1, ...), custom_call_target="tpu_custom_call" | custom-call | flops 25999998976 | bytes 41943040 | tf_op jit(solution)/shard_map/pallas_call | solution.py:530
  105.7 2.2 %copy.13 = bf16[64,7168]{1,0:T(8,128)(2,1)} copy(bf16[64,7168]{1,0:T(8,128)(2,1)} %shard_map.109) | data formatting | bytes 1835008

commit v4 on v3

--- a/solution.py
+++ b/solution.py
@@ -202,8 +202,8 @@
 
 
 schedule = {
-    0: ["spread"], 2: ["near"], 4: ["far"], 5: ["pass1"], 6: ["pass2"], 7: ["pass3"], 8: ["tail0"], 9: ["tail1"],
-    11: ["open", "weights"], 13: ["side"], 14: ["across"],
+    0: ["spread"], 1: ["near"], 2: ["far"], 3: ["pass1", "pass2"], 4: ["pass3", "tail0"], 5: ["tail1"],
+    6: ["open", "weights"], 7: ["side", "across"],
 }
 
 
@@ -334,12 +334,12 @@
 def layer_kernel(
     len_ref, live_ref, q_hbm, qr_hbm, lat_hbm, rope_hbm, new_ref, newr_ref, anc_ref, up_ref, proj_ref,
     out_hbm,
-    q_ref, raw_s, qr_ref, lat_ref, rope_ref, top_s, tot_s, acc_s, turn_s, ctx_s, all_ref, blk_ref,
+    q_ref, raw_s, qr_ref, lat_ref, rope_ref, tree_s, tree_rope_s, bias_s, turn_s, ctx_s, all_ref, blk_ref,
     hv, act, part, relay, sums, near, fin, got,
     send, recv, local, loads, writes,
 ):
     factor = score_scale * log2_e
-    heads, width, key_blk, sub = 64, 512, 1024, 256
+    heads, width, sub = 64, 512, 256
     m = Mover(send, recv)
     plan = gather_plan(m, up_ref, proj_ref, all_ref, blk_ref, local)
     project = Project(m, out_hbm, ctx_s, all_ref, blk_ref, hv, act, part, relay, sums, near, fin, got, writes)
@@ -384,76 +384,67 @@
             copy.start()
         fetch_ropes(r).start()
     plan["first"]()
+    arrange_ropes(0)
+    tree_s[...] = jnp.zeros(tree_s.shape, jnp.bfloat16)
+    tree_rope_s[...] = jnp.zeros(tree_rope_s.shape, jnp.bfloat16)
+    bias_s[...] = jnp.full(bias_s.shape, very_negative, jnp.float32)
+    tree_s[:, pl.ds(0, 32), :] = new_ref[...]
+    tree_rope_s[:, pl.ds(0, 32), pl.ds(0, 64)] = newr_ref[...]
+    bias_s[:, :, pl.ds(0, 32)] = jnp.where(anc_ref[...] > 0, 0.0, very_negative)
     for r in range(2):
         position = lax.broadcasted_iota(jnp.int32, (64, 2048), 1)
         row = lax.broadcasted_iota(jnp.int32, (64, 2048), 0)
         outside = jnp.logical_and(row == 0, position >= len_ref[r])
-        arrange_ropes(r)
         rope_ref[r, pl.ds(64, 64), :] = jnp.where(outside, very_negative, 0.0).astype(jnp.bfloat16)
 
     def step(i, carry):
         for r in range(2):
-            @pl.when(i == r * 8)
+            @pl.when(i == r * 4)
             def _():
+                if r:
+                    arrange_ropes(r)
                 for copy in fetch(r):
                     copy.wait()
 
-        request = i // 8
-        block = lax.rem(i, 8) // 2
-        key = lax.rem(i, 2)
+        request = i // 4
+        block = lax.rem(i, 4)
         row0 = block * 8
 
         def queries(part):
             start = pl.multiple_of(row0 * heads + part * sub, sub)
             return q_ref[request, pl.ds(start, sub), :], qr_ref[request, pl.ds(start, sub), :]
 
-        @pl.when(key == 0)
-        def _():
-            for part in range(2):
-                q, qr = queries(part)
-                rows = pl.ds(part * sub, sub)
-                s = lax.dot_general(q, new_ref[request], nt, preferred_element_type=jnp.float32)
-                s = s + lax.dot_general(qr[:, :64], newr_ref[request], nt, preferred_element_type=jnp.float32)
-                s = s * factor
-                anc = anc_ref[request, pl.ds(row0 + part * 4, 4), :]
-                bias = jnp.where(anc > 0, 0.0, very_negative)
-                s = (s.reshape(4, heads, 32) + bias[:, None, :]).reshape(sub, 32)
-                top = jnp.max(s, axis=1, keepdims=True)
-                w = jnp.exp2(s - top)
-                top_s[rows, :] = jnp.broadcast_to(top, (sub, 128))
-                tot_s[rows, :] = jnp.where(lax.broadcasted_iota(jnp.int32, (sub, 128), 1) == 0,
-                                           jnp.sum(w, axis=1, keepdims=True), 0.0)
-                acc_s[rows, :] = jnp.dot(w.astype(jnp.bfloat16), new_ref[request], preferred_element_type=jnp.float32)
-
-        offset = pl.multiple_of(key * key_blk, key_blk)
-        keys = lat_ref[request, pl.ds(offset, key_blk), :]
-        rope_keys = rope_ref[request, :, pl.ds(offset, key_blk)]
-        scores = []
-        for part in range(2):
+        keys = lat_ref[request]
+        rope_keys = rope_ref[request]
+
+        def scores(part):
             q, qr = queries(part)
-            scores.append(lax.dot_general(q, keys, nt, preferred_element_type=jnp.float32)
-                          + jnp.dot(qr, rope_keys, preferred_element_type=jnp.float32))
-        for part in range(2):
-            s = scores[part]
-            rows = pl.ds(part * sub, sub)
-            old = top_s[rows, :]
-            new = jnp.maximum(old, jnp.max(s, axis=1, keepdims=True) * factor)
-            rescale = jnp.exp2(old - new)
-            w = jnp.exp2(s * factor - new[:, :1])
-            tot_s[rows, :] = tot_s[rows, :] * rescale + lane_sum(w)
-            top_s[rows, :] = new
-            acc_s[rows, :] = acc_s[rows, :] * rescale[:, :1] + jnp.dot(
-                w.astype(jnp.bfloat16), keys, preferred_element_type=jnp.float32)
-
-        @pl.when(key == 1)
-        def _():
-            total = jnp.sum(tot_s[...], axis=1, keepdims=True)
-            ctx = (acc_s[...] * (1.0 / total)).reshape(8, heads, width)
-            alive = row0 + lax.broadcasted_iota(jnp.int32, (8, heads, 1), 0) < live_ref[request]
-            ctx = jnp.where(alive, ctx, 0.0)
-            turn_s[:, pl.ds(pl.multiple_of(row0, 8), 8), :] = jnp.swapaxes(ctx, 0, 1)
-
-        @pl.when(i == 7)
+            return (lax.dot_general(q, keys, nt, preferred_element_type=jnp.float32)
+                    + jnp.dot(qr, rope_keys, preferred_element_type=jnp.float32))
+
+        def tree_scores(part):
+            q, qr = queries(part)
+            s = (lax.dot_general(q, tree_s[request], nt, preferred_element_type=jnp.float32)
+                 + lax.dot_general(qr, tree_rope_s[request], nt, preferred_element_type=jnp.float32))
+            bias = bias_s[request, pl.ds(row0 + part * 4, 4), :]
+            return (s.reshape(4, heads, 128) + bias[:, None, :]).reshape(sub, 128)
+
+        both = [(scores(part), tree_scores(part)) for part in range(2)]
+        done = []
+        for part, (s, t) in enumerate(both):
+            top = jnp.maximum(jnp.max(s, axis=1, keepdims=True), jnp.max(t, axis=1, keepdims=True)) * factor
+            w = jnp.exp2(s * factor - top)
+            v = jnp.exp2(t * factor - top)
+            total = jnp.sum(lane_sum(w) + v, axis=1, keepdims=True)
+            acc = (jnp.dot(w.astype(jnp.bfloat16), keys, preferred_element_type=jnp.float32)
+                   + jnp.dot(v.astype(jnp.bfloat16), tree_s[request], preferred_element_type=jnp.float32))
+            ctx = (acc * (1.0 / total)).reshape(4, heads, width)
+            alive = row0 + part * 4 + lax.broadcasted_iota(jnp.int32, (4, heads, 1), 0) < live_ref[request]
+            done.append(jnp.where(alive, ctx, 0.0))
+        ctx = jnp.concatenate(done, axis=0)
+        turn_s[:, pl.ds(pl.multiple_of(row0, 8), 8), :] = jnp.swapaxes(ctx, 0, 1)
+
+        @pl.when(i == 3)
         def _():
             ctx_s[...] = turn_s[...].astype(jnp.bfloat16)
 
@@ -464,7 +455,7 @@
                     plan[name]()
         return carry
 
-    lax.fori_loop(0, 16, step, 0)
+    lax.fori_loop(0, 8, step, 0)
     ctx_s[...] = turn_s[...].astype(jnp.bfloat16)
     p = project
     p.open(1)
@@ -538,9 +529,9 @@
             pltpu.VMEM((2, 2048, 128), bf),
             pltpu.VMEM((2, 2048, 512), bf),
             pltpu.VMEM((2, 128, 2048), bf),
-            pltpu.VMEM((512, 128), jnp.float32),
-            pltpu.VMEM((512, 128), jnp.float32),
-            pltpu.VMEM((512, 512), jnp.float32),
+            pltpu.VMEM((2, 128, 512), bf),
+            pltpu.VMEM((2, 128, 128), bf),
+            pltpu.VMEM((2, 32, 128), jnp.float32),
             pltpu.VMEM((64, 32, 512), jnp.float32),
             pltpu.VMEM((64, 32, 512), bf),
             pltpu.VMEM((16, 4, 512, 128), bf),

time: 109 us -> 105 us (0.963)
  Pallas kernels: 106 us -> 103 us
    pallas_call x1, Pallas kernels: 106 us -> 103 us  [layer(): pl.pallas_call(layer_kernel, out_shape=jax.ShapeDtypeStruct((64, 7168), b...]
where the time goes in v4:
time: 105 us
  Pallas kernels  103 us (98%)
  local copies, waits for them, and re-layouts  2.16 us (2%)
    pallas_call x1, Pallas kernels, layer(): pl.pallas_call(layer_kernel, out_shape=jax.ShapeDtypeStruct((64, 7168), b...  103 us
    unnamed x1, local copies, waits for them, and re-layouts  2.16 us

profile of v4, /device:TPU:0, one launch (start us, length us, event | category | flops | bytes accessed | tf_op | source)
XLA Modules:
  0.0 104.7 jit_solution(6098139747907009228)
XLA Ops:
  0.0 102.6 %shard_map.109 = bf16[64,7168]{1,0:T(8,128)(2,1)} custom-call(s32[2]{0:T(128)} %len_ref.1, s32[2]{0:T(128)} %live_ref.1, bf16[2,2048,512]{2,1,0:T(8,128)(2,1)} %bitcast.1, bf16[2,32,4096]{2,1,0:T(8,128)(2,1)} %qr_hbm.1, bf16[2,2048,512]{2,1,0:T(8,128)(2,1)} %lat_hbm.1, bf16[2,64,2048]{2,1,0:T(8,128)(2,1)} %rope_hbm.1, bf16[2,32,512]{2,1,0:T(8,128)(2,1)} %new_ref.1, ...), custom_call_target="tpu_custom_call" | custom-call | flops 25999998976 | bytes 41943040 | tf_op jit(solution)/shard_map/pallas_call | solution.py:521
  102.6 2.2 %copy.13 = bf16[64,7168]{1,0:T(8,128)(2,1)} copy(bf16[64,7168]{1,0:T(8,128)(2,1)} %shard_map.109) | data formatting | bytes 1835008

commit v5 on v4

--- a/solution.py
+++ b/solution.py
@@ -219,9 +219,9 @@
 
 
 class Project:
-    def __init__(self, m, out_hbm, ctx, up, blk, hv, act, part, relay, sums, near, fin, got, writes):
-        self.m, self.out_hbm, self.ctx, self.up, self.blk, self.hv, self.act, self.part = (
-            m, out_hbm, ctx, up, blk, hv, act, part)
+    def __init__(self, m, out_hbm, turn, up, blk, hv, act, part, relay, sums, near, fin, got, writes):
+        self.m, self.out_hbm, self.turn, self.up, self.blk, self.hv, self.act, self.part = (
+            m, out_hbm, turn, up, blk, hv, act, part)
         self.relay, self.sums, self.near, self.fin, self.got, self.writes = relay, sums, near, fin, got, writes
 
         def copy(src, i, dst, j, **step):
@@ -249,11 +249,11 @@
 
         def heads(i, carry):
             h = kb * 16 + i
-            v = jnp.dot(self.ctx[h], self.up[h // 4, lax.rem(h, 4)], preferred_element_type=jnp.float32)
+            v = jnp.dot(self.turn[q, h].astype(jnp.bfloat16), self.up[h // 4, lax.rem(h, 4)], preferred_element_type=jnp.float32)
             target[:, pl.ds(pl.multiple_of(i * 128, 128), 128)] = v.astype(jnp.bfloat16)
             return carry
 
-        lax.fori_loop(0, 16, heads, 0, unroll=4)
+        lax.fori_loop(0, 16, heads, 0, unroll=8)
 
     def open(self, q):
         for dx in (1, 3, 2):
@@ -334,7 +334,7 @@
 def layer_kernel(
     len_ref, live_ref, q_hbm, qr_hbm, lat_hbm, rope_hbm, new_ref, newr_ref, anc_ref, up_ref, proj_ref,
     out_hbm,
-    q_ref, raw_s, qr_ref, lat_ref, rope_ref, tree_s, tree_rope_s, bias_s, turn_s, ctx_s, all_ref, blk_ref,
+    q_ref, raw_s, qr_ref, lat_ref, rope_ref, tree_s, tree_rope_s, bias_s, turn_s, all_ref, blk_ref,
     hv, act, part, relay, sums, near, fin, got,
     send, recv, local, loads, writes,
 ):
@@ -342,7 +342,7 @@
     heads, width, sub = 64, 512, 256
     m = Mover(send, recv)
     plan = gather_plan(m, up_ref, proj_ref, all_ref, blk_ref, local)
-    project = Project(m, out_hbm, ctx_s, all_ref, blk_ref, hv, act, part, relay, sums, near, fin, got, writes)
+    project = Project(m, out_hbm, turn_s, all_ref, blk_ref, hv, act, part, relay, sums, near, fin, got, writes)
 
     def begin():
         plan["ready"]()
@@ -365,13 +365,13 @@
 
         def pair(i, carry):
             both = raw_s[r, :, pl.ds(pl.multiple_of(i * 128, 128), 128)].astype(jnp.float32)
-            turn_s[2 * i, :, pl.ds(0, 128)] = jnp.where(lane < 64, both, after)
-            turn_s[2 * i + 1, :, pl.ds(0, 128)] = jnp.where(lane < 64, pltpu.roll(both, 64, 1), after)
+            turn_s[r, 2 * i, :, pl.ds(0, 128)] = jnp.where(lane < 64, both, after)
+            turn_s[r, 2 * i + 1, :, pl.ds(0, 128)] = jnp.where(lane < 64, pltpu.roll(both, 64, 1), after)
             return carry
 
         lax.fori_loop(0, heads // 2, pair, 0, unroll=4)
         for block in range(4):
-            turned = jnp.swapaxes(turn_s[:, pl.ds(block * 8, 8), pl.ds(0, 128)], 0, 1)
+            turned = jnp.swapaxes(turn_s[r, :, pl.ds(block * 8, 8), pl.ds(0, 128)], 0, 1)
             qr_ref[r, pl.ds(block * 512, 512), :] = turned.reshape(512, 128).astype(jnp.bfloat16)
 
     def fetch(r):
@@ -442,11 +442,7 @@
             alive = row0 + part * 4 + lax.broadcasted_iota(jnp.int32, (4, heads, 1), 0) < live_ref[request]
             done.append(jnp.where(alive, ctx, 0.0))
         ctx = jnp.concatenate(done, axis=0)
-        turn_s[:, pl.ds(pl.multiple_of(row0, 8), 8), :] = jnp.swapaxes(ctx, 0, 1)
-
-        @pl.when(i == 3)
-        def _():
-            ctx_s[...] = turn_s[...].astype(jnp.bfloat16)
+        turn_s[request, :, pl.ds(pl.multiple_of(row0, 8), 8), :] = jnp.swapaxes(ctx, 0, 1)
 
         for point, names in schedule.items():
             @pl.when(i == point)
@@ -456,7 +452,6 @@
         return carry
 
     lax.fori_loop(0, 8, step, 0)
-    ctx_s[...] = turn_s[...].astype(jnp.bfloat16)
     p = project
     p.open(1)
     plan["block_ready"]()
@@ -532,8 +527,7 @@
             pltpu.VMEM((2, 128, 512), bf),
             pltpu.VMEM((2, 128, 128), bf),
             pltpu.VMEM((2, 32, 128), jnp.float32),
-            pltpu.VMEM((64, 32, 512), jnp.float32),
-            pltpu.VMEM((64, 32, 512), bf),
+            pltpu.VMEM((2, 64, 32, 512), jnp.float32),
             pltpu.VMEM((16, 4, 512, 128), bf),
             pltpu.VMEM((2, 4, 512, 896), bf),
             pltpu.VMEM((2, 4, 32, 2048), bf),

time: 105 us -> 105 us (level); the launches traced: 105 us -> 104 us
  Pallas kernels: 103 us -> 101 us
    pallas_call x1, Pallas kernels: 103 us -> 101 us  [layer(): pl.pallas_call(layer_kernel, out_shape=jax.ShapeDtypeStruct((64, 7168), b...]
where the time goes in v5:
time: 105 us; the launch traced here: 104 us
  Pallas kernels  101 us (96%)
  local copies, waits for them, and re-layouts  2.16 us (2%)
    pallas_call x1, Pallas kernels, layer(): pl.pallas_call(layer_kernel, out_shape=jax.ShapeDtypeStruct((64, 7168), b...  101 us
    unnamed x1, local copies, waits for them, and re-layouts  2.16 us

profile of v5, /device:TPU:0, one launch (start us, length us, event | category | flops | bytes accessed | tf_op | source)
XLA Modules:
  0.0 103.6 jit_solution(2218182653960931010)
XLA Ops:
  0.0 101.5 %shard_map.109 = bf16[64,7168]{1,0:T(8,128)(2,1)} custom-call(s32[2]{0:T(128)} %len_ref.1, s32[2]{0:T(128)} %live_ref.1, bf16[2,2048,512]{2,1,0:T(8,128)(2,1)} %bitcast.1, bf16[2,32,4096]{2,1,0:T(8,128)(2,1)} %qr_hbm.1, bf16[2,2048,512]{2,1,0:T(8,128)(2,1)} %lat_hbm.1, bf16[2,64,2048]{2,1,0:T(8,128)(2,1)} %rope_hbm.1, bf16[2,32,512]{2,1,0:T(8,128)(2,1)} %new_ref.1, ...), custom_call_target="tpu_custom_call" | custom-call | flops 25999998976 | bytes 41943040 | tf_op jit(solution)/shard_map/pallas_call | solution.py:516
  101.5 2.2 %copy.13 = bf16[64,7168]{1,0:T(8,128)(2,1)} copy(bf16[64,7168]{1,0:T(8,128)(2,1)} %shard_map.109) | data formatting | bytes 1835008
